TPU v7x, 32 devices: a whole 2x2x4 slice. The times are simulated.
32 devices in a mesh: seq: 16 (over z, y, x), head: 2 (over core).
Axes of the slice: x: 2, y: 2, z: 4, core: 2. Of those that a mesh axis runs over, the one named last changes fastest.
Arguments:
- tokens: bfloat16 [32768, 512], P(('seq', 'head')), may hold values from -6 to 6
- first_values: bfloat16 [32768, 256], P(('seq', 'head')), may hold values from -6 to 6
- cotangent: bfloat16 [32768, 512], P(('seq', 'head')), may hold values from -6 to 6
- slot_count: int32 [16], P('seq'), may hold values from 1 to 8, as said below
- seq_lengths: int32 [16, 8], P('seq'), may hold values from 129 to 2048, as said below
- query_weight: bfloat16 [512, 512], replicated, may hold values from -0.5 to 0.5
- key_weight: bfloat16 [512, 512], replicated, may hold values from -0.25 to 0.25
- value_weight: bfloat16 [512, 256], replicated, may hold values from -0.25 to 0.25
- mixing_weight: bfloat16 [512, 512], replicated, may hold values from -1 to 1
- expand_weight: bfloat16 [512, 2048], replicated, may hold values from -0.25 to 0.25
- shrink_weight: bfloat16 [2048, 512], replicated, may hold values from -0.125 to 0.125
- expand_bias: float32 [2048], replicated, may hold values from -3 to 3
- before_gain: float32 [512], replicated, may hold values from 0.5 to 1.5
- before_shift: float32 [512], replicated, may hold values from -2 to 2
- middle_gain: float32 [512], replicated, may hold values from 0.5 to 1.5
- middle_shift: float32 [512], replicated, may hold values from -2 to 2
Outputs:
- output: bfloat16 [32768, 512], P(('seq', 'head'))
- input_grad: bfloat16 [32768, 512], P(('seq', 'head'))
- skip_grad: bfloat16 [32768, 256], P(('seq', 'head'))
- query_grad: float32 [512, 512], replicated
- key_grad: float32 [512, 512], replicated
- value_grad: float32 [512, 256], replicated
- mixing_grad: float32 [512, 512], replicated
- expand_grad: float32 [512, 2048], replicated
- shrink_grad: float32 [2048, 512], replicated
- bias_grad: float32 [2048], replicated
- before_gain_grad: float32 [512], replicated
- before_shift_grad: float32 [512], replicated
- middle_gain_grad: float32 [512], replicated
- middle_shift_grad: float32 [512], replicated
Inputs may be any that keep to these rules, and one draw needn't show every extreme that they name: `slot_count`: each bucket holds 1, 2, 4 or 8 sequences; the first bucket holds one and the second eight. `seq_lengths`: for a bucket of c sequences each slot below c holds a length above 2048 / (2 c) and at most 2048 / c; slots from c on are not read. The first bucket's sequence has 2048 tokens.
All inputs are finite; a program needn't handle non-finite values.
Results may differ from a plain program's by a relative error of at most 0.013.
The roundings to bfloat16 on the way count: a program that leaves them out, or rounds other values in their place, can miss the bound.
Values may be sent and summed in bfloat16 or wider, within the bound.
No kernel may reach another device: no remote copies, remote signals or barrier semaphores. Data moves between devices by JAX's collectives and lax.ppermute only.
A program may use at most 256 MiB of HBM per device.

v0:
```python
from functools import partial
import math
import jax
import jax.numpy as jnp
from jax import lax
from jax.experimental import pallas as pl
from jax.experimental.pallas import tpu as pltpu
from jax.sharding import PartitionSpec as P

BLOCK = 256
SLOT_OPTIONS = (1, 2, 4, 8)
LOG2E = math.log2(math.e)
F32, BF16 = jnp.float32, jnp.bfloat16
MASKED = -1e30
EPS = 1e-05
MIB = 1 << 20
VMEM_MIB, WHOLE_MIB = 56, 62


def nn(a, b):
    return lax.dot_general(a, b, (((1,), (0,)), ((), ())), preferred_element_type=F32)


def nt(a, b):
    return lax.dot_general(a, b, (((1,), (1,)), ((), ())), preferred_element_type=F32)


def tn(a, b):
    return lax.dot_general(a, b, (((0,), (0,)), ((), ())), preferred_element_type=F32)


def sorter(count, transposed=False):
    each = BLOCK // count
    grouped = lax.broadcasted_iota(jnp.int32, (BLOCK, BLOCK), 1 if transposed else 0)
    plain = lax.broadcasted_iota(jnp.int32, (BLOCK, BLOCK), 0 if transposed else 1)
    place = (plain & (count - 1)) * each + (plain >> (count.bit_length() - 1))
    return jnp.where(grouped == place, 1.0, 0.0).astype(BF16)


def store_grouped(write, values, tile, total, count):
    each = BLOCK // count
    for group in range(count):
        start = pl.multiple_of(group * (total // count) + tile * each, each)
        write(pl.ds(start, each), values[group * each : (group + 1) * each])


def load_grouped(read, tile, total, count):
    each = BLOCK // count
    parts = []
    for group in range(count):
        start = pl.multiple_of(group * (total // count) + tile * each, each)
        parts.append(read(pl.ds(start, each)))
    return parts[0] if count == 1 else jnp.concatenate(parts, axis=0)


def normalized(rows):
    average = jnp.mean(rows, axis=-1, keepdims=True)
    centred = rows - average
    spread = jnp.mean(centred * centred, axis=-1, keepdims=True)
    scale = lax.rsqrt(spread + EPS)
    return centred * scale, scale


def as_columns(vectors):
    stack = jnp.concatenate(vectors + [jnp.zeros((128 - len(vectors), vectors[0].shape[1]), F32)], axis=0)
    return jnp.transpose(stack).astype(BF16)


def forward_kernel(
    info, own_in, other_in, skip_own_in, skip_other_in, query_in, key_in, value_in, gain_in, shift_in,
    mixed_own_out, mixed_other_out, query_out, keys_out, saved_out, mixed_out, logsum_out, normed_out,
    own, other, skip_own, skip_other, query_weight, key_weight, value_weight,
    mixed_own, mixed_other, query, keys, saved, mixed, logsum, normed, values, gain, shift, semaphores,
):
    count, head = info[0], info[1]
    half = own.shape[0]
    total = 2 * half
    blocks = total // BLOCK
    cols = pl.ds(pl.multiple_of(head * 256, 256), 256)
    fresh_cols = pl.ds(pl.multiple_of(head * 128, 128), 128)
    mover = Mover(semaphores)
    mover.start(own_in, own, "own")
    mover.start(gain_in, gain, "gain")
    mover.start(shift_in, shift, "shift")
    mover.start(query_in.at[:, cols], query_weight, "q")
    mover.start(key_in.at[:, cols], key_weight, "k")
    mover.start(value_in.at[:, fresh_cols], value_weight, "v")
    mover.start(skip_own_in.at[:, fresh_cols], skip_own, "skip")
    values[:, :, 128:] = jnp.ones((2, total, 128), BF16)

    for rows_ref, skip_ref, which, needs in (
        (own, skip_own, head, ("own", "gain", "shift", "q", "k", "v", "skip")),
        (other, skip_other, 1 - head, ("other", "skip_other")),
    ):
        mover.wait(*needs)
        if needs[0] == "own":
            mover.start(other_in, other, "other")
            mover.start(skip_other_in.at[:, fresh_cols], skip_other, "skip_other")

        def project(step, _, rows_ref=rows_ref, skip_ref=skip_ref, which=which):
            at = pl.ds(pl.multiple_of(step * BLOCK, BLOCK), BLOCK)
            tile = which * (half // BLOCK) + step
            hat, _s = normalized(rows_ref[at, :].astype(F32))
            low = (hat * gain[...] + shift[...]).astype(BF16)
            skip = skip_ref[at, :]

            def put(count_here):
                rows, skipped = low, skip
                if count_here > 1:
                    order = sorter(count_here)
                    rows = nn(order, low).astype(BF16)
                    skipped = nn(order, skip).astype(BF16)
                q = nn(rows, query_weight[...]).astype(BF16)
                q = (q.astype(F32) * (0.125 * LOG2E)).astype(BF16)
                k = nn(rows, key_weight[...]).astype(BF16)
                f = nn(rows, value_weight[...]).astype(BF16)

                def put_in(ref, part, value):
                    def write(dst, piece):
                        if part is None:
                            ref[dst, :] = piece
                        else:
                            ref[part, dst, :128] = piece
                            if ref is values:
                                saved[part, dst, :] = piece

                    store_grouped(write, value, tile, total, count_here)

                put_in(normed, None, rows)
                put_in(query, 0, q[:, :128])
                put_in(query, 1, q[:, 128:])
                put_in(keys, 0, k[:, :128])
                put_in(keys, 1, k[:, 128:])
                put_in(values, 0, f)
                put_in(values, 1, skipped)

            for option in SLOT_OPTIONS:
                pl.when(count == option)(partial(put, option))
            return 0

        lax.fori_loop(0, half // BLOCK, project, 0)

    for source, target in ((query, query_out), (keys, keys_out), (saved, saved_out), (normed, normed_out)):
        mover.start(source, target)

    per_slot = blocks // count
    lane = lax.broadcasted_iota(jnp.int32, (1, 128), 1)
    tri = lax.broadcasted_iota(jnp.int32, (BLOCK, BLOCK), 1) <= lax.broadcasted_iota(
        jnp.int32, (BLOCK, BLOCK), 0
    )

    def attend(block, _):
        width = block % per_slot + 1
        here = pl.multiple_of(block * BLOCK, BLOCK)

        def run(wide):
            first = pl.multiple_of((block - (wide - 1)) * BLOCK, BLOCK)

            def score(h):
                pair, sub = h // 2, h % 2
                q = query[pair, pl.ds(here, BLOCK), :]
                qm = jnp.where((lane < 64) == (sub == 0), q, jnp.zeros_like(q))
                diag = nt(qm, keys[pair, pl.ds(here, BLOCK), :])
                rest = None
                if wide > 1:
                    rest = nt(qm, keys[pair, pl.ds(first, (wide - 1) * BLOCK), :])
                return diag, rest

            def soften(diag, rest):
                diag = jnp.where(tri, diag, MASKED)
                top = jnp.max(diag, axis=1, keepdims=True)
                if wide > 1:
                    top = jnp.maximum(top, jnp.max(rest, axis=1, keepdims=True))
                raised = [jnp.exp2(diag - top).astype(BF16)]
                if wide > 1:
                    raised.append(jnp.exp2(rest - top).astype(BF16))
                return top, raised

            def finish(h, top, raised):
                acc = nn(raised[0], values[h // 2, pl.ds(here, BLOCK), :])
                if wide > 1:
                    acc += nn(raised[1], values[h // 2, pl.ds(first, (wide - 1) * BLOCK), :])
                sums = acc[:, 128:]
                return acc[:, :128] / sums, jnp.transpose(top + jnp.log2(sums))[0:1, :]

            scores = [score(h) for h in range(4)]
            softened = [soften(*scores[h]) for h in range(4)]
            outs = [finish(h, *softened[h]) for h in range(4)]
            for pair in range(2):
                mixed[pair, pl.ds(here, BLOCK), :] = jnp.where(lane < 64, outs[2*pair][0], outs[2*pair+1][0]).astype(BF16)
                for sub in range(2):
                    logsum[pair, sub : sub + 1, pl.ds(here, BLOCK)] = outs[2*pair+sub][1]

        for wide in range(1, blocks + 1):
            pl.when(width == wide)(partial(run, wide))
        return 0

    lax.fori_loop(0, blocks, attend, 0)
    mover.start(mixed, mixed_out)
    mover.start(logsum, logsum_out)

    for out_ref, target, which in (
        (mixed_other, mixed_other_out, 1 - head),
        (mixed_own, mixed_own_out, head),
    ):

        def give(step, _, out_ref=out_ref, which=which):
            at = pl.ds(pl.multiple_of(step * BLOCK, BLOCK), BLOCK)
            tile = which * (half // BLOCK) + step

            def put(count_here):
                for pair in range(2):
                    part = load_grouped(lambda s: mixed[pair, s, :], tile, total, count_here)
                    if count_here > 1:
                        part = nn(sorter(count_here, True), part).astype(BF16)
                    out_ref[at, pair * 128 : (pair + 1) * 128] = part

            for option in SLOT_OPTIONS:
                pl.when(count == option)(partial(put, option))
            return 0

        lax.fori_loop(0, half // BLOCK, give, 0)
        mover.start(out_ref, target)
    mover.wait_all()


class Mover:
    def __init__(self, semaphores):
        self.semaphores, self.used, self.open = semaphores, 0, {}

    def start(self, source, target, name=None):
        copy = pltpu.make_async_copy(source, target, self.semaphores.at[self.used])
        copy.start()
        self.open[self.used if name is None else name] = copy
        self.used += 1

    def wait(self, *names):
        for name in names:
            self.open.pop(name).wait()

    def wait_all(self):
        self.wait(*list(self.open))


def run_kernel(kernel, name, scalars, args, outs, scratch, moves, flops, aliases=None, limit=VMEM_MIB):
    smem = pl.BlockSpec(memory_space=pltpu.SMEM)
    large = pl.BlockSpec(memory_space=pl.ANY)
    size = lambda shape, dtype: math.prod(shape) * jnp.dtype(dtype).itemsize
    moved = sum(size(a.shape, a.dtype) for a in args) + sum(size(*o) for o in outs)
    return pl.pallas_call(
        kernel,
        in_specs=[smem] * len(scalars) + [large] * len(args),
        out_specs=[large] * len(outs),
        out_shape=[jax.ShapeDtypeStruct(*o) for o in outs],
        scratch_shapes=[pltpu.VMEM(*s) for s in scratch] + [pltpu.SemaphoreType.DMA((moves,))],
        input_output_aliases=aliases or {},
        cost_estimate=pl.CostEstimate(flops=flops, bytes_accessed=moved, transcendentals=0),
        compiler_params=pltpu.CompilerParams(vmem_limit_bytes=limit * MIB),
        name=name,
    )(*scalars, *args)


def forward_attention(info, own, other, skip_own, skip_other, wq, wk, wv, gain, shift):
    half, width = own.shape
    total = 2 * half
    group = wq.shape[1] // 2
    outs = [
        ((half, group), BF16),
        ((half, group), BF16),
        ((2, total, 128), BF16),
        ((2, total, 128), BF16),
        ((2, total, 128), BF16),
        ((2, total, 128), BF16),
        ((2, 8, total), F32),
        ((total, width), BF16),
    ]
    scratch = [
        ((half, width), BF16),
        ((half, width), BF16),
        ((half, 128), BF16),
        ((half, 128), BF16),
        ((width, group), BF16),
        ((width, group), BF16),
        ((width, 128), BF16),
        *outs,
        ((2, total, 256), BF16),
        (gain.shape, F32),
        (shift.shape, F32),
    ]
    return run_kernel(
        forward_kernel, "forward_attention", (info,),
        (own, other, skip_own, skip_other, wq, wk, wv, gain, shift), outs, scratch, 17, 10 * 10**9,
        limit=WHOLE_MIB,
    )


COLS = 512
TILE, PART = 512, 256
GELU_SLOPE = math.sqrt(2.0 / math.pi)
GELU_CUBE = 0.044715


def gelu_pair(v):
    square = v * v
    bend = jnp.tanh(v * (GELU_SLOPE + (GELU_SLOPE * GELU_CUBE) * square))
    front = 0.5 + 0.5 * bend
    steep = v * (2.0 * GELU_SLOPE + (6.0 * GELU_SLOPE * GELU_CUBE) * square)
    return v * front, front + steep * (front * (1.0 - front))


def rows_kernel(
    info, lengths, tokens_in, mixed_own_in, mixed_other_in, cotangent_in, mixing_in, expand_in,
    shrink_in, bias_in, gain_in, shift_in,
    output_out, after_grad_out, send_own_out, send_other_out,
    own_stay_out, own_away_out, other_stay_out, other_away_out, vectors_out,
    tokens, mixed_own, mixed_other, cotangent, mixing_weight, expand_weight, shrink_weight,
    expand_bias, gain, shift, output, after_grad, send_own, send_other, grads_own, grads_other,
    vectors, bias_grad, gain_grads, active, pre_grad, middle, out_grad, after_low, semaphores,
):
    mover = Mover(semaphores)
    for source, target, name in (
        (mixing_in, mixing_weight, "mixing"),
        (tokens_in, tokens, "tokens"),
        (mixed_own_in, mixed_own, "own"),
        (mixed_other_in, mixed_other, "other"),
        (gain_in, gain, "gain"),
        (shift_in, shift, "shift"),
        (bias_in, expand_bias, "bias"),
        (expand_in, expand_weight, "expand"),
        (shrink_in, shrink_weight, "shrink"),
        (cotangent_in, cotangent, "cotangent"),
    ):
        mover.start(source, target, name)
    count, head = info[0], info[1]
    half, width = tokens.shape
    hidden = expand_weight.shape[1]
    group = mixed_own.shape[1]
    shift_by = (
        (count >= 2).astype(jnp.int32)
        + (count >= 4).astype(jnp.int32)
        + (count >= 8).astype(jnp.int32)
    )
    here = pl.ds(pl.multiple_of(head * group, group), group)
    there = pl.ds(pl.multiple_of((1 - head) * group, group), group)
    bias_grad[...] = jnp.zeros_like(bias_grad)
    gain_grads[...] = jnp.zeros_like(gain_grads)
    mover.wait("mixing", "tokens", "own", "other", "gain", "shift", "bias")

    def tile(step, _):
        at = pl.ds(pl.multiple_of(step * TILE, TILE), TILE)
        row = head * half + step * TILE + lax.broadcasted_iota(jnp.int32, (TILE, 1), 0)
        slot = row & (count - 1)
        limit = jnp.zeros_like(row)
        for s in range(lengths.shape[0]):
            limit = jnp.where(slot == s, lengths[s], limit)
        valid = (row >> shift_by) < limit

        def first_wait(*names):
            pl.when(step == 0)(lambda: mover.wait(*names))

        after = (
            tokens[at, :].astype(F32)
            + nn(mixed_own[at, :], mixing_weight[here, :])
            + nn(mixed_other[at, :], mixing_weight[there, :])
        )
        hat, scale = normalized(after)
        low = (hat * gain[...] + shift[...]).astype(BF16)
        middle[at, :] = low
        first_wait("expand", "shrink", "cotangent")
        grad_out = jnp.where(valid, cotangent[at, :].astype(F32), 0.0)
        grad_low = grad_out.astype(BF16)
        out_grad[at, :] = grad_low

        def products(c):
            cs = slice(c, c + PART)
            return nn(low, expand_weight[:, cs]), nt(grad_low, shrink_weight[cs, :])

        ahead = products(0)
        for c in range(0, hidden, PART):
            cs = slice(c, c + PART)
            now = ahead
            if c + PART < hidden:
                ahead = products(c + PART)
            act, slope = gelu_pair(now[0] + expand_bias[:, cs])
            active[at, cs] = act.astype(BF16)
            g = now[1] * slope
            bias_grad[0:1, cs] += jnp.sum(g, axis=0, keepdims=True)
            pre_grad[at, cs] = g.astype(BF16)
        g_middle = nt(pre_grad[at, :], expand_weight[...])
        grown = nn(active[at, :], shrink_weight[...])
        gain_grads[0:1, :] += jnp.sum(g_middle * hat, axis=0, keepdims=True)
        gain_grads[1:2, :] += jnp.sum(g_middle, axis=0, keepdims=True)
        y = g_middle * gain[...]
        g_after = grad_out + scale * (
            y
            - jnp.mean(y, axis=-1, keepdims=True)
            - hat * jnp.mean(y * hat, axis=-1, keepdims=True)
        )
        after_grad[at, :] = g_after
        g_low = g_after.astype(BF16)
        after_low[at, :] = g_low
        output[at, :] = jnp.where(valid, after + grown, 0.0).astype(BF16)
        send_own[at, :] = nt(g_low, mixing_weight[here, :]).astype(BF16)
        send_other[at, :] = nt(g_low, mixing_weight[there, :]).astype(BF16)
        return 0

    lax.fori_loop(0, half // TILE, tile, 0)

    for source, target in (
        (send_other, send_other_out),
        (send_own, send_own_out),
        (output, output_out),
        (after_grad, after_grad_out),
    ):
        mover.start(source, target)
    vectors[...] = jnp.zeros_like(vectors)
    for n, c in enumerate(range(0, hidden, width)):
        vectors[n : n + 1, :] = bias_grad[0:1, c : c + width]
    vectors[4:6, :] = gain_grads[0:2, :]
    mover.start(vectors, vectors_out)
    first_half = grads_own.shape[0] // 2
    for grads, stay_out, away_out, mixed, which, side in (
        (grads_other, other_stay_out, other_away_out, mixed_other, 1 - head, info[4]),
        (grads_own, own_stay_out, own_away_out, mixed_own, head, info[2]),
    ):
        stay = pl.ds(pl.multiple_of(side * first_half, 16), first_half)
        away = pl.ds(pl.multiple_of((1 - side) * first_half, 16), first_half)

        def weights(step, _, grads=grads, which=which):
            cs = pl.ds(pl.multiple_of((2 * which + step) * COLS, COLS), COLS)
            at = pl.multiple_of(step * COLS, COLS)
            grads[pl.ds(at, COLS), :] = tn(active[:, cs], out_grad[...]).astype(BF16)
            grads[pl.ds(2 * COLS + at, COLS), :] = tn(middle[...], pre_grad[:, cs]).astype(BF16)
            return 0

        lax.fori_loop(0, 2, weights, 0)
        grads[4 * COLS :, :] = tn(mixed[...], after_low[...]).astype(BF16)
        mover.start(grads.at[away], away_out)
        mover.start(grads.at[stay], stay_out)
    mover.wait_all()


def row_part(info, lengths, tokens, mixed_own, mixed_other, cotangent, wo, we, ws, bias, gain, shift):
    half, width = tokens.shape
    hidden = we.shape[1]
    group = mixed_own.shape[1]
    outs = [
        ((half, width), BF16),
        ((half, width), F32),
        ((half, group), BF16),
        ((half, group), BF16),
        *[(((hidden + group) // 2, width), BF16)] * 4,
        ((8, width), F32),
    ]
    args = (tokens, mixed_own, mixed_other, cotangent, wo, we, ws, bias, gain, shift)
    scratch = [
        *[(a.shape, a.dtype) for a in args],
        *outs[:4],
        ((hidden + group, width), BF16),
        ((hidden + group, width), BF16),
        outs[8],
        ((8, hidden), F32),
        ((8, width), F32),
        ((half, hidden), BF16),
        ((half, hidden), BF16),
        ((half, width), BF16),
        ((half, width), BF16),
        ((half, width), BF16),
    ]
    return run_kernel(
        rows_kernel, "row_part", (info, lengths), args, outs, scratch, 19, 15 * 10**9,
        limit=WHOLE_MIB,
    )


def arrange_gradient(count, head, grad_own, grad_other, mixed, grad, inner):
    half = grad_own.shape[0]
    total = 2 * half

    for rows_ref, which in ((grad_own, head), (grad_other, 1 - head)):

        def arrange(step, _, rows_ref=rows_ref, which=which):
            at = pl.ds(pl.multiple_of(step * BLOCK, BLOCK), BLOCK)
            tile = which * (half // BLOCK) + step
            rows = rows_ref[at, :]

            def put(count_here):
                value = rows
                if count_here > 1:
                    value = nn(sorter(count_here), rows).astype(BF16)
                for pair in range(2):

                    def write(dst, piece, pair=pair):
                        grad[pair, dst, :] = piece

                    store_grouped(
                        write, value[:, pair * 128 : (pair + 1) * 128], tile, total, count_here
                    )

            for option in SLOT_OPTIONS:
                pl.when(count == option)(partial(put, option))
            return 0

        lax.fori_loop(0, half // BLOCK, arrange, 0)

    def inners(block, _):
        at = pl.ds(pl.multiple_of(block * BLOCK, BLOCK), BLOCK)
        for pair in range(2):
            flipped = jnp.transpose(grad[pair, at, :].astype(F32) * mixed[pair, at, :].astype(F32))
            for sub in range(2):
                inner[pair, sub : sub + 1, at] = jnp.sum(
                    flipped[sub * 64 : (sub + 1) * 64], axis=0, keepdims=True
                )
        return 0

    lax.fori_loop(0, total // BLOCK, inners, 0)


def attend_blocks(
    count, first, last, query, keys, values, grad, logsum, inner, query_total, kept, key_sums, value_sums
):
    blocks = first + query.shape[1] // BLOCK
    per_slot = blocks // count
    lane = lax.broadcasted_iota(jnp.int32, (1, 128), 1)
    tri = lax.broadcasted_iota(jnp.int32, (BLOCK, BLOCK), 0) <= lax.broadcasted_iota(
        jnp.int32, (BLOCK, BLOCK), 1
    )

    def attend(block, _):
        more = per_slot - block % per_slot - 1
        here = pl.multiple_of((block - first) * BLOCK, BLOCK)
        at = pl.ds(here, BLOCK)

        def part(start, size, diagonal):
            span = pl.ds(pl.multiple_of(start, BLOCK), size)

            def score(h):
                pair, sub = h // 2, h % 2
                pick = (lane < 64) == (sub == 0)
                k, v = keys[pair, at, :], values[pair, at, :]
                k = jnp.where(pick, k, jnp.zeros_like(k))
                v = jnp.where(pick, v, jnp.zeros_like(v))
                return k, nt(k, query[pair, span, :]), nt(v, grad[pair, span, :])

            def finish(h, k, raw, grad_probs):
                pair, sub = h // 2, h % 2
                probs = jnp.exp2(raw - logsum[pair, sub : sub + 1, span])
                if diagonal:
                    probs = jnp.where(tri, probs, 0.0)
                grad_scores = (probs * (grad_probs - inner[pair, sub : sub + 1, span])).astype(BF16)
                grad_value = nn(probs.astype(BF16), grad[pair, span, :])
                grad_key = nn(grad_scores, query[pair, span, :])
                if diagonal:
                    value_sums[h], key_sums[h] = grad_value, grad_key
                else:
                    value_sums[h] += grad_value
                    key_sums[h] += grad_key
                return tn(grad_scores, k)

            ahead = score(0)
            done = []
            for h in range(4):
                now = ahead
                if h < 3:
                    ahead = score(h + 1)
                done.append(finish(h, *now))
                if h % 2:
                    query_total[h // 2, span, :] += done[h - 1] + done[h]

        part(here, BLOCK, True)

        def two(n, _):
            part(here + BLOCK + n * (2 * BLOCK), 2 * BLOCK, False)
            return 0

        lax.fori_loop(0, more // 2, two, 0)

        @pl.when(more % 2 == 1)
        def _():
            part(here + more * BLOCK, BLOCK, False)

        for pair in range(2):
            for start, sums, scale in ((0, key_sums, 1.0 / LOG2E), (256, value_sums, 1.0)):
                picked = jnp.where(lane < 64, sums[2 * pair], sums[2 * pair + 1])
                kept[at, start + pair * 128 : start + (pair + 1) * 128] = (picked * scale).astype(BF16)
        return 0

    lax.fori_loop(first, last, attend, 0)


def arrange_kernel(
    info, grad_own_in, grad_other_in, mixed_in, grad_out, inner_out,
    grad_own, grad_other, mixed, grad, inner, semaphores,
):
    mover = Mover(semaphores)
    for source, target in ((grad_own_in, grad_own), (grad_other_in, grad_other), (mixed_in, mixed)):
        mover.start(source, target)
    mover.wait_all()
    arrange_gradient(info[0], info[1], grad_own, grad_other, mixed, grad, inner)
    mover.start(grad, grad_out)
    mover.start(inner, inner_out)
    mover.wait_all()


def arrange_rows(info, grad_own, grad_other, mixed):
    total = mixed.shape[1]
    outs = [((2, total, 128), BF16), ((2, 8, total), F32)]
    args = (grad_own, grad_other, mixed)
    scratch = [(a.shape, BF16) for a in args] + outs
    return run_kernel(arrange_kernel, "arrange_rows", (info,), args, outs, scratch, 5, 10**8, limit=WHOLE_MIB)


def fetch_blocks(mover, first, last, sources, targets):
    query, keys, values, grad, logsum, inner, *before = sources
    total = query.shape[1]
    span, rows = pl.ds(first * BLOCK, total - first * BLOCK), pl.ds(first * BLOCK, (last - first) * BLOCK)
    for source, target in zip(
        (
            keys.at[:, rows], query.at[:, span], values.at[:, rows], grad.at[:, span],
            logsum.at[:, :, span], inner.at[:, :, span], *[b.at[:, span] for b in before],
        ),
        targets,
    ):
        mover.start(source, target)


def next_kernel(first, last, info, *refs):
    count = 7 if first else 6
    sources, (query_total_out, kept_out), local, (key_sums, value_sums, kept, semaphores) = (
        refs[:count], refs[count : count + 2], refs[count + 2 : count + 9], refs[count + 9 :]
    )
    mover = Mover(semaphores)
    fetch_blocks(mover, first, last, sources, local)
    keys, query, values, grad, logsum, inner, query_total = local
    if not first:
        query_total[...] = jnp.zeros_like(query_total)
    mover.wait_all()
    attend_blocks(
        info[0], first, last, query, keys, values, grad, logsum, inner, query_total, kept,
        key_sums, value_sums,
    )
    total = sources[0].shape[1]
    span = pl.ds(first * BLOCK, total - first * BLOCK)
    mover.start(query_total, query_total_out.at[:, span])
    mover.start(kept, kept_out)
    mover.wait_all()


def local_blocks(first, last, total):
    rows, span = (last - first) * BLOCK, total - first * BLOCK
    return [
        ((2, rows, 128), BF16),
        ((2, span, 128), BF16),
        ((2, rows, 128), BF16),
        ((2, span, 128), BF16),
        ((2, 8, span), F32),
        ((2, 8, span), F32),
        ((2, span, 128), F32),
        ((4, BLOCK, 128), F32),
        ((4, BLOCK, 128), F32),
    ]


def next_blocks(first, last, info, before, query, keys, values, grad, logsum, inner):
    outs = [(query.shape, F32), (((last - first) * BLOCK, 512), BF16)]
    args = (query, keys, values, grad, logsum, inner) + ((before,) if first else ())
    return run_kernel(
        partial(next_kernel, first, last), f"blocks_{first}", (info,), args, outs,
        local_blocks(first, last, query.shape[1]) + [outs[1]], 9, 5 * 10**9, {7: 0} if first else {},
    )


def last_kernel(first, pieces, info, *refs):
    sources, refs = refs[:7], refs[7:]
    normed_in, gain_in, shift_in, vectors_in, query_in, key_in, value_in = refs[:7]
    kept_in, refs = refs[7 : 7 + pieces], refs[7 + pieces :]
    stay_out, away_out, packed_out = refs[:3]
    local, (key_sums, value_sums, *refs) = refs[3:10], refs[10:]
    kept, normed, gain, shift, vectors, query_weight, key_weight, value_weight, before, weight_grad, packed, semaphores = refs
    keys, query, values, grad, logsum, inner, query_total = local
    total = packed.shape[0]
    head = info[1]
    cols = pl.ds(pl.multiple_of(head * 256, 256), 256)
    fresh_cols = pl.ds(pl.multiple_of(head * 128, 128), 128)
    mover = Mover(semaphores)
    fetch_blocks(mover, first, total // BLOCK, sources, local)
    mover.start(sources[6].at[:, pl.ds(0, first * BLOCK)], before, "before")
    mover.start(normed_in, normed, "normed")
    mover.start(vectors_in, vectors, "vectors")
    mover.start(gain_in, gain, "gain")
    mover.start(shift_in, shift, "shift")
    mover.start(query_in.at[:, cols], query_weight, "q")
    mover.start(key_in.at[:, cols], key_weight, "k")
    mover.start(value_in.at[:, fresh_cols], value_weight, "v")
    row = 0
    for n, piece in enumerate(kept_in):
        mover.start(piece, packed.at[pl.ds(row, piece.shape[0]), pl.ds(256, 512)], f"p{n}")
        row += piece.shape[0]
    mover.wait(*range(7))
    attend_blocks(
        info[0], first, total // BLOCK, query, keys, values, grad, logsum, inner, query_total, kept,
        key_sums, value_sums,
    )
    mover.wait_all()
    packed[row:, 256:] = kept[...]
    for pair in range(2):
        lanes = slice(pair * 128, (pair + 1) * 128)
        packed[:row, lanes] = (before[pair, :, :] * 0.125).astype(BF16)
        packed[row:, lanes] = (query_total[pair, :, :] * 0.125).astype(BF16)
    mover.start(packed, packed_out)
    ones = jnp.ones((8, total), BF16)
    gain_grad = jnp.zeros((gain.shape[1], 1), F32)
    shift_grad = jnp.zeros((gain.shape[1], 1), F32)
    gain_column = jnp.transpose(jnp.broadcast_to(gain[...], (128, gain.shape[1])))[:, :1]
    shift_column = jnp.transpose(jnp.broadcast_to(shift[...], (128, gain.shape[1])))[:, :1]
    for start, stop, weight in ((0, 256, query_weight), (256, 512, key_weight), (512, 640, value_weight)):
        part = packed[:, start:stop]
        product = tn(normed[...], part)
        sums = nn(ones, part)[0:1, :]
        weight_grad[:, start:stop] = product.astype(BF16)
        weight = weight[...].astype(F32)
        shift_grad += jnp.sum(weight * sums, axis=1, keepdims=True)
        gain_grad += jnp.sum(weight * (product - shift_column * sums), axis=1, keepdims=True)
    lane = lax.broadcasted_iota(jnp.int32, (1, 128), 1)
    edge = jnp.where(lane == 0, gain_grad / gain_column, jnp.where(lane == 1, shift_grad, 0.0))
    stack = jnp.concatenate([vectors[...], jnp.zeros((120, vectors.shape[1]), F32)], axis=0)
    edge += jnp.where(lane >= 8, pltpu.roll(jnp.transpose(stack), 8, 1), 0.0)
    weight_grad[:, 640:] = edge.astype(BF16)
    rows = weight_grad.shape[0] // 2
    mover.start(weight_grad.at[pl.ds(pl.multiple_of((1 - info[3]) * rows, 16), rows)], away_out)
    mover.start(weight_grad.at[pl.ds(pl.multiple_of(info[3] * rows, 16), rows)], stay_out)
    mover.wait_all()


def last_blocks(first, info, before, query, keys, values, grad, logsum, inner, normed, gain, shift, vectors, wq, wk, wv, kept):
    total, width = normed.shape
    outs = [((width // 2, 768), BF16), ((width // 2, 768), BF16), ((total, 768), BF16)]
    scratch = local_blocks(first, total // BLOCK, total) + [
        ((total - first * BLOCK, 512), BF16),
        (normed.shape, BF16),
        (gain.shape, F32),
        (shift.shape, F32),
        (vectors.shape, F32),
        ((width, 256), BF16),
        ((width, 256), BF16),
        ((width, 128), BF16),
        ((2, first * BLOCK, 128), F32),
        ((width, 768), BF16),
        outs[2],
    ]
    return run_kernel(
        partial(last_kernel, first, len(kept)), "last_blocks", (info,),
        (query, keys, values, grad, logsum, inner, before, normed, gain, shift, vectors, wq, wk, wv, *kept),
        outs, scratch, 18 + len(kept), 5 * 10**9,
    )


def back_kernel(
    info, packed_in, query_in, key_in, value_in, back_own_out, back_other_out, skip_own_out, skip_other_out,
    packed, query_weight, key_weight, value_weight, back_own, back_other, skip_own, skip_other, back, semaphores,
):
    count, head = info[0], info[1]
    total = packed.shape[0]
    half = total // 2
    cols = pl.ds(pl.multiple_of(head * 256, 256), 256)
    fresh_cols = pl.ds(pl.multiple_of(head * 128, 128), 128)
    mover = Mover(semaphores)
    mover.start(packed_in, packed)
    mover.start(query_in.at[:, cols], query_weight)
    mover.start(key_in.at[:, cols], key_weight)
    mover.start(value_in.at[:, fresh_cols], value_weight)
    mover.wait_all()

    def close(block, _):
        at = pl.ds(pl.multiple_of(block * BLOCK, BLOCK), BLOCK)
        back[at, :] = (
            nt(packed[at, :256], query_weight[...])
            + nt(packed[at, 256:512], key_weight[...])
            + nt(packed[at, 512:640], value_weight[...])
        ).astype(BF16)
        return 0

    lax.fori_loop(0, total // BLOCK, close, 0)

    for back_ref, skip_ref, back_out, skip_out, which in (
        (back_other, skip_other, back_other_out, skip_other_out, 1 - head),
        (back_own, skip_own, back_own_out, skip_own_out, head),
    ):

        def give(step, _, back_ref=back_ref, skip_ref=skip_ref, which=which):
            at = pl.ds(pl.multiple_of(step * BLOCK, BLOCK), BLOCK)
            tile = which * (half // BLOCK) + step

            def put(count_here):
                g = load_grouped(lambda s: back[s, :], tile, total, count_here)
                k = load_grouped(lambda s: packed[s, 640:], tile, total, count_here)
                if count_here > 1:
                    order = sorter(count_here, True)
                    g = nn(order, g).astype(BF16)
                    k = nn(order, k).astype(BF16)
                back_ref[at, :] = g
                skip_ref[at, :] = k

            for option in SLOT_OPTIONS:
                pl.when(count == option)(partial(put, option))
            return 0

        lax.fori_loop(0, half // BLOCK, give, 0)
        mover.start(back_ref, back_out)
        mover.start(skip_ref, skip_out)
    mover.wait_all()


def back_rows(info, packed, wq, wk, wv):
    total, width = packed.shape[0], wq.shape[0]
    half = total // 2
    outs = [((half, width), BF16), ((half, width), BF16), ((half, 128), BF16), ((half, 128), BF16)]
    scratch = [
        (packed.shape, BF16),
        ((width, 256), BF16),
        ((width, 256), BF16),
        ((width, 128), BF16),
        *outs,
        ((total, width), BF16),
    ]
    return run_kernel(
        back_kernel, "back_rows", (info,), (packed, wq, wk, wv), outs, scratch, 8, 2 * 10**9
    )


def close_kernel(
    info, tokens_in, after_grad_in, back_own_in, back_other_in, kept_in, arrived_in, gain_in,
    result_out, skip_out,
    tokens, after_grad, back_own, back_other, gain, result, skip_grad, semaphores,
):
    head = info[1]
    mover = Mover(semaphores)
    mover.start(gain_in, gain)
    mover.start(tokens_in, tokens)
    mover.start(after_grad_in, after_grad)
    mover.start(back_own_in, back_own)
    mover.start(back_other_in, back_other)
    mover.start(kept_in, skip_grad.at[:, pl.ds(pl.multiple_of(head * 128, 128), 128)])
    mover.start(arrived_in, skip_grad.at[:, pl.ds(pl.multiple_of((1 - head) * 128, 128), 128)])
    mover.wait_all()
    mover.start(skip_grad, skip_out)

    def tile(step, _):
        at = pl.ds(pl.multiple_of(step * BLOCK, BLOCK), BLOCK)
        hat, scale = normalized(tokens[at, :].astype(F32))
        y = (back_own[at, :].astype(F32) + back_other[at, :].astype(F32)) * gain[...]
        result[at, :] = (
            after_grad[at, :]
            + scale
            * (
                y
                - jnp.mean(y, axis=-1, keepdims=True)
                - hat * jnp.mean(y * hat, axis=-1, keepdims=True)
            )
        ).astype(BF16)
        return 0

    lax.fori_loop(0, tokens.shape[0] // BLOCK, tile, 0)
    mover.start(result, result_out)
    mover.wait_all()


def close_rows(info, tokens, after_grad, back_own, back_other, kept, arrived, gain):
    args = (tokens, after_grad, back_own, back_other, kept, arrived, gain)
    outs = [(tokens.shape, BF16), ((tokens.shape[0], 256), BF16)]
    scratch = [(a.shape, a.dtype) for a in args[:4]] + [(gain.shape, F32)] + outs
    return run_kernel(close_kernel, "close_rows", (info,), args, outs, scratch, 9, 10**8)


def unpack_kernel(late, info, *refs):
    half_in, refs = refs[0], refs[1 + (3 if late else 0) :]
    shrink_out, expand_out, mixing_out, half, wide, semaphores = refs
    which = 1 - info[1] if late else info[1]
    width = half.shape[1]
    top = 4 * COLS + mixing_out.shape[0] // 2
    mover = Mover(semaphores)
    for at in range(0, 4 * COLS, COLS):
        mover.start(half_in.at[pl.ds(at, COLS)], half.at[pl.ds(at, COLS)], at)
    mover.start(half_in.at[pl.ds(4 * COLS, half.shape[0] - 4 * COLS)], half.at[pl.ds(4 * COLS, half.shape[0] - 4 * COLS)], "rest")
    for at in range(0, 4 * COLS, COLS):
        mover.wait(at)
        wide[at : at + COLS, :] = half[at : at + COLS, :].astype(F32)
        if at < 2 * COLS:
            row = pl.multiple_of(which * 2 * COLS + at, COLS)
            mover.start(wide.at[pl.ds(at, COLS)], shrink_out.at[pl.ds(row, COLS)])
        else:
            col = pl.multiple_of(which * 2 * COLS + at - 2 * COLS, COLS)
            mover.start(wide.at[pl.ds(at, COLS)], expand_out.at[:, pl.ds(col, COLS)])
    mover.wait("rest")
    wide[4 * COLS :, :] = half[4 * COLS :, :].astype(F32)
    row = pl.multiple_of(which * (top - 4 * COLS), 256)
    mover.start(wide.at[pl.ds(4 * COLS, top - 4 * COLS)], mixing_out.at[pl.ds(row, top - 4 * COLS)])
    mover.wait_all()


def unpack_half(info, half, before=()):
    rows, width = half.shape
    hidden = 4 * COLS
    outs = [((hidden, width), F32), ((width, hidden), F32), ((width, width), F32)]
    scratch = [(half.shape, BF16), ((rows, width), F32)]
    return run_kernel(
        partial(unpack_kernel, bool(before)), "unpack_late" if before else "unpack_half", (info,),
        (half, *before), outs, scratch, 10, 10**8, {2 + n: n for n in range(3)} if before else {},
        limit=20,
    )


def split_kernel(
    info, mine_in, arrived_in, query_out, key_out, value_out, *refs
):
    vectors_out, (mine, arrived, query, key, value), vectors, semaphores = refs[:5], refs[5:10], refs[10:15], refs[15]
    head = info[1]
    mover = Mover(semaphores)
    mover.start(mine_in, mine)
    mover.start(arrived_in, arrived)
    mover.wait_all()
    for half, which in ((mine, head), (arrived, 1 - head)):
        for target, wide, at in ((query, 256, 0), (key, 256, 256), (value, 128, 512)):
            cols = pl.ds(pl.multiple_of(which * wide, 128), wide)
            target[:, cols] = half[:, at : at + wide].astype(F32)
    for source, target in ((query, query_out), (key, key_out), (value, value_out)):
        mover.start(source, target)
    edges = jnp.transpose(mine[:, 640:].astype(F32) + arrived[:, 640:].astype(F32))
    gain, shift, bias, middle_gain, middle_shift = vectors
    width = gain.shape[1]
    for target, at in ((gain, 0), (shift, 1), (middle_gain, 12), (middle_shift, 13)):
        target[...] = edges[at : at + 1]
    for n in range(bias.shape[1] // width):
        bias[:, n * width : (n + 1) * width] = edges[8 + n : 9 + n]
    for source, target in zip(vectors, vectors_out):
        mover.start(source, target)
    mover.wait_all()


def split_projection(info, mine, arrived):
    width = mine.shape[0]
    outs = [((width, 512), F32), ((width, 512), F32), ((width, 256), F32)]
    outs += [((1, n * width), F32) for n in (1, 1, 4, 1, 1)]
    scratch = [(mine.shape, BF16), (mine.shape, BF16)] + outs
    return run_kernel(split_kernel, "split_projection", (info,), (mine, arrived), outs, scratch, 10, 10**8, limit=20)


def swap_cores(array):
    return lax.ppermute(array, "head", [(0, 1), (1, 0)])


def half_of(array, which):
    rows = array.shape[0] // 2
    return lax.dynamic_slice_in_dim(array, which * rows, rows, 0)


def add_low(a, b):
    return (a.astype(F32) + b.astype(F32)).astype(BF16)


def join(mine, theirs, which):
    both = jnp.concatenate([mine, mine], axis=0)
    return lax.dynamic_update_slice_in_dim(both, theirs, (1 - which) * mine.shape[0], 0)


def after_all(first, *rest):
    return lax.optimization_barrier((first, *rest))


class SeqSum:
    def __init__(self, orders):
        self.size = lax.axis_size("seq")
        bits = self.size.bit_length() - 1
        self.orders = [
            [b for b in order if b < bits] + [b for b in range(bits) if b not in order]
            for order in orders
        ]
        self.stage, self.bits = 0, bits
        self.fitting, self.whole, self.kept = False, False, None

    def begin(self, stay, stay_come, away, away_come):
        self.mine, self.coming, self.half = stay, stay_come, None if stay_come is None else -1
        self.sent = away if away_come is None else add_low(away, away_come)
        self.next, self.stage, self.trail = 0, 1, [0]

    def which(self, stage, other=0):
        bit = jnp.where(lax.axis_index("head") == other, self.orders[0][stage], self.orders[1][stage])
        return (lax.axis_index("seq") >> bit) & 1

    def swap(self, array, stage):
        pairs = []
        for i in range(self.size):
            for core in range(2):
                pairs.append((2 * i + core, 2 * (i ^ (1 << self.orders[core][stage])) + core))
        return lax.ppermute(array, ("seq", "head"), pairs)

    def added(self, which=None):
        parts = [a if which is None else half_of(a, which) for a in (self.mine, self.coming) if a is not None]
        return parts[0] if len(parts) == 1 else add_low(*parts)

    def prepare(self):
        if self.stage < self.bits:
            self.settle()
            if self.stage < self.bits - 1 and self.mine.shape[0] % 32 == 0:
                which = self.which(self.stage)
                self.trail.append(self.stage)
                self.sent, self.half = self.added(1 - which), which
            else:
                self.sent = self.mine = self.added()
                self.coming = None
            self.next = self.stage
            self.stage += 1
            return True
        self.settle()
        if self.fitting:
            self.mine = join(self.mine, self.coming, self.which(self.next))
        else:
            self.mine, self.fitting = self.added(), True
        if not self.trail:
            return False
        self.next, self.sent = self.trail.pop(), self.mine
        return True

    def launch(self):
        self.kept = self.coming
        self.coming = self.swap(self.sent, self.next)

    def settle(self):
        if self.half is not None:
            parts = [a for a in (self.mine, self.kept) if a is not None]
            if not isinstance(self.half, int):
                parts = [half_of(a, self.half) for a in parts]
            self.mine = parts[0] if len(parts) == 1 else add_low(*parts)
            self.half = None

    def via(self, stage):
        return lambda array: self.swap(array, stage)

    def flow(self, ready, small):
        while ready or self.stage < self.bits or len(self.trail) > 3:
            if not ready:
                self.prepare()
            ready = False
            (came,) = yield [(self.via(self.next), self.sent)]
            self.kept, self.coming = self.coming, came
        self.settle()
        piece = join(self.mine, self.coming, self.which(self.next)) if self.fitting else self.added()
        far, mid, near = self.trail
        rows = piece.shape[0]
        came_near, got_own = yield [(self.via(near), piece), (self.via(far), piece)]
        both = join(piece, came_near, self.which(near))
        if small:
            came_mid, got_near = yield [(self.via(mid), both), (self.via(far), came_near)]
            self.mine = join(both, came_mid, self.which(mid))
            got_mid, other_mine = yield [(self.via(far), came_mid), (swap_cores, self.mine)]
        else:
            (came_mid,) = yield [(self.via(mid), both)]
            cut = rows // 32 * 16
            (first,) = yield [(self.via(far), jnp.concatenate([came_near, came_mid[:cut]], axis=0))]
            (second,) = yield [(self.via(far), came_mid[cut:])]
            got_near, got_mid = first[:rows], jnp.concatenate([first[rows:], second], axis=0)
            self.mine = join(both, came_mid, self.which(mid))
        theirs = join(join(got_own, got_near, self.which(near)), got_mid, self.which(mid))
        self.mine = join(self.mine, theirs, self.which(far))
        self.whole = True
        if small:
            (other_theirs,) = yield [(swap_cores, theirs)]
            self.other = join(other_mine, other_theirs, self.which(far, 1))
        else:
            (self.other,) = yield [(swap_cores, self.mine)]


ORDERS = ((0, 1, 2, 3), (1, 2, 3, 0))
PROJECTION_ORDERS = ((0, 1, 2, 3), (1, 0, 2, 3))
CUTS = (0, 2, 4, 6, 8)


def on_device(
    tokens, first_values, cotangent, slot_count, seq_lengths, query_weight, key_weight, value_weight,
    mixing_weight, expand_weight, shrink_weight, expand_bias, before_gain, before_shift,
    middle_gain, middle_shift,
):
    head = lax.axis_index("head")
    sums, projection = SeqSum(ORDERS), SeqSum(PROJECTION_ORDERS)
    info = jnp.stack([slot_count[0], head, sums.which(0), projection.which(0), sums.which(0, 1)])
    info = info.astype(jnp.int32)
    lengths = seq_lengths[0]
    row = lambda v: v.reshape(1, -1)

    other = swap_cores(tokens)
    skip_other = swap_cores(first_values)
    mixed_own, mixed_away, query, keys, values, mixed, logsum, normed = forward_attention(
        info, tokens, other, first_values, skip_other, query_weight, key_weight, value_weight,
        row(before_gain), row(before_shift),
    )
    mixed_other = swap_cores(mixed_away)
    output, after_grad, grad_own, grad_away, own_stay, own_away, other_stay, other_away, row_vectors = row_part(
        info, lengths, tokens, mixed_own, mixed_other, cotangent, mixing_weight, expand_weight,
        shrink_weight, row(expand_bias), row(middle_gain), row(middle_shift),
    )
    grad_other = swap_cores(grad_away)
    grad_other, other_away = after_all(grad_other, other_away)
    away_come = swap_cores(other_away)
    grad, inner = arrange_rows(info, grad_own, grad_other, mixed)
    grad, away_come = after_all(grad, away_come)
    sums.begin(own_stay, swap_cores(other_stay), own_away, away_come)
    attention = (query, keys, values, grad, logsum, inner)
    query_total, pieces = None, []
    for first, last in zip(CUTS, CUTS[1:]):
        if first > 0:
            sums.prepare()
        *attention, sums.sent = after_all(*attention, sums.sent)
        sums.launch()
        if last < CUTS[-1]:
            query_total, kept = next_blocks(first, last, info, query_total, *attention)
            pieces.append(kept)
            query_total, sums.coming, sums.mine, sums.kept = after_all(
                query_total, sums.coming, sums.mine, sums.kept
            )
        else:
            projection_stay, projection_away, packed = last_blocks(
                first, info, query_total, *attention, normed, row(before_gain), row(before_shift),
                row_vectors, query_weight, key_weight, value_weight, pieces,
            )
            packed, sums.coming, sums.mine, sums.kept = after_all(packed, sums.coming, sums.mine, sums.kept)
    projection.begin(projection_stay, None, projection_away, None)

    lanes = [projection.flow(True, True), sums.flow(False, False)]
    pending = [next(lane) for lane in lanes]
    work, made, extra, finished = 0, None, (), False
    while pending:
        inputs = ()
        if work == 0:
            inputs, kernel = (packed,), lambda p: back_rows(info, p, query_weight, key_weight, value_weight)
        elif work == 1:
            extra = (back_away, skip_away)
        elif work == 2:
            inputs, kernel = (back_other, skip_arrived), lambda b, k: close_rows(
                info, tokens, after_grad, back_own, b, skip_own, k, row(before_gain)
            )
        elif sums.whole and made is None:
            inputs, kernel = (sums.mine,), lambda m: unpack_half(info, m)
        elif made is not None and not finished:
            inputs, kernel, finished = (sums.other, *made), lambda o, *m: unpack_half(info, o, tuple(m)), True
        moves = [move for group in pending for move in group]
        tied = after_all(*[array for _, array in moves], *extra, *inputs)
        count = len(moves)
        came = [swap(a) for (swap, _), a in zip(moves, tied)]
        came += [swap_cores(a) for a in tied[count : count + len(extra)]]
        results = kernel(*tied[count + len(extra) :]) if inputs else ()
        tied = after_all(*came, *results)
        came, results = tied[: len(came)], tied[len(came) :]
        if work == 0:
            back_own, back_away, skip_own, skip_away = results
        elif work == 1:
            back_other, skip_arrived = came[count:]
        elif work == 2:
            input_grad, skip_grad = results
        elif results:
            made = results
        work, extra = work + 1, ()
        later = []
        came = list(came)
        for lane, group in zip(lanes, pending):
            mine, came = came[: len(group)], came[len(group) :]
            try:
                later.append((lane, lane.send(mine)))
            except StopIteration:
                pass
        lanes, pending = [lane for lane, _ in later], [p for _, p in later]
    if made is None:
        made = unpack_half(info, sums.mine)
    if not finished:
        made = unpack_half(info, sums.other, tuple(made))
    shrink_grad, expand_grad, mixing_grad = made
    query_grad, key_grad, value_grad, *edges = split_projection(info, projection.mine, projection.other)
    before_gain_grad, before_shift_grad, bias_grad, middle_gain_grad, middle_shift_grad = [
        v.reshape(-1) for v in edges
    ]
    return (
        output, input_grad, skip_grad, query_grad, key_grad, value_grad, mixing_grad, expand_grad,
        shrink_grad, bias_grad, before_gain_grad, before_shift_grad, middle_gain_grad, middle_shift_grad,
    )


def solution(mesh):
    rows = P(("seq", "head"), None)
    return jax.shard_map(
        on_device,
        mesh=mesh,
        in_specs=(rows, rows, rows, P("seq"), P("seq", None)) + (P(),) * 11,
        out_specs=(rows, rows, rows) + (P(),) * 11,
        check_vma=False,
    )
```

profile of v0, /device:TPU:0, one launch (start us, length us, event | category | flops | bytes accessed | tf_op | source)
XLA Modules:
  0.0 192.1 jit_solution(9432645553649333952)
XLA Ops:
  2.5 1.9 collective-permute-done.1.skip_other_in
  5.6 22.1 %forward_attention.1 = (bf16[1024,256]{1,0:T(8,128)(2,1)}, bf16[1024,256]{1,0:T(8,128)(2,1)}, bf16[2,2048,128]{2,1,0:T(8,128)(2,1)}, bf16[2,2048,128]{2,1,0:T(8,...) custom-call(s32[5]{0:T(128)} %stack.16.info, ...), custom_call_target="tpu_custom_call" | custom-call | flops 10000000000 | bytes 11931648 | tf_op jit(solution)/shard_map/forward_attention/pallas_call | solution.py:250
  28.1 1.7 collective-permute-done.2.mixed_other_in
  30.6 25.7 %row_part.1 = (bf16[1024,512]{1,0:T(8,128)(2,1)}, f32[1024,512]{1,0:T(8,128)}, bf16[1024,256]{1,0:T(8,128)(2,1)}, bf16[1024,256]{1,0:T(8,128)(2,1)}, bf16[1152,5...) custom-call(s32[5]{0:T(128)} %stack.16.info, ...), custom_call_target="tpu_custom_call" | custom-call | flops 15000000512 | bytes 16805888 | tf_op jit(solution)/shard_map/row_part/pallas_call | solution.py:250
  56.8 1.8 collective-permute-done.3.grad_other_in
  59.3 4.6 %arrange_rows.1 = (bf16[2,2048,128]{2,1,0:T(8,128)(2,1)}, f32[2,8,2048]{2,1,0:T(8,128)}) custom-call(s32[5]{0:T(128)} %stack.16.info, bf16[1024,256]{1,0:T(8,128)(2,1)} %get-tuple-element.171.grad_own_in, bf16[1024,256]{1,0:T(8,128)(2,1)} %copy-done.3, bf16[2,2048,128]{2,1,0:T(8,128)(2,1)} %get-tuple-element.175.mixed_in), custom_call_target="tpu_custom_call" | custom-call | flops 100000000 | bytes 3276800 | tf_op jit(solution)/shard_map/arrange_rows/pallas_call | solution.py:250
  64.0 1.9 %add_convert_fusion.1 = bf16[1152,512]{1,0:T(8,128)(2,1)S(1)} fusion(bf16[1152,512]{1,0:T(8,128)(2,1)} %collective-permute-done.4, bf16[1152,512]{1,0:T(8,128)(2,1)} %get-tuple-element.181), kind=kLoop, calls=%fused_computation.2 | loop fusion | flops 2359296 | bytes 3538944 | tf_op jit(solution)/shard_map/convert_element_type | solution.py:958
  67.0 16.4 %blocks_0.1 = (f32[2,2048,128]{2,1,0:T(8,128)}, bf16[512,512]{1,0:T(8,128)(2,1)}) custom-call(s32[5]{0:T(128)} %stack.16.info, bf16[2,2048,128]{2,1,0:T(8,128)(2,1)} %get-tuple-element.220.refs_0_, bf16[2,2048,128]{2,1,0:T(8,128)(2,1)} %get-tuple-element.221.refs_1_, bf16[2,2048,128]{2,1,0:T(8,128)(2,1)} %get-tuple-element.222.refs_2_, ...), custom_call_target="tpu_custom_call" | custom-call | flops 5000000000 | bytes 7077888 | tf_op jit(solution)/shard_map/blocks_0/pallas_call | solution.py:250
  83.8 1.2 add_convert_fusion.3
  85.0 1.2 collective-permute-start.7
  86.3 13.2 %blocks_2.1 = (f32[2,2048,128]{2,1,0:T(8,128)}, bf16[512,512]{1,0:T(8,128)(2,1)}) custom-call(s32[5]{0:T(128)} %stack.16.info, bf16[2,2048,128]{2,1,0:T(8,128)(2,1)} %get-tuple-element.220.refs_0_, bf16[2,2048,128]{2,1,0:T(8,128)(2,1)} %get-tuple-element.221.refs_1_, ...), custom_call_target="tpu_custom_call", output_to_operand_aliasing={{0}: (7, {})} | custom-call | flops 5000000000 | bytes 9175040 | tf_op jit(solution)/shard_map/blocks_2/pallas_call | solution.py:250
  100.9 9.5 %blocks_4.1 = (f32[2,2048,128]{2,1,0:T(8,128)}, bf16[512,512]{1,0:T(8,128)(2,1)}) custom-call(s32[5]{0:T(128)} %stack.16.info, bf16[2,2048,128]{2,1,0:T(8,128)(2,1)} %get-tuple-element.220.refs_0_, bf16[2,2048,128]{2,1,0:T(8,128)(2,1)} %get-tuple-element.221.refs_1_, ...), custom_call_target="tpu_custom_call", output_to_operand_aliasing={{0}: (7, {})} | custom-call | flops 5000000000 | bytes 9175040 | tf_op jit(solution)/shard_map/blocks_4/pallas_call | solution.py:250
  110.9 2.3 %collective-permute-start.9 = (bf16[288,512]{1,0:T(8,128)(2,1)S(1)}, bf16[288,512]{1,0:T(8,128)(2,1)S(1)}, u32[]{:S(2)}, u32[]{:S(2)}) collective-permute-start(bf16[288,512]{1,0:T(8,128)(2,1)S(1)} %add_convert_fusion.5), channel_id=1, source_target_pairs={{0,16},{1,3},{2,18},{3,1},{4,20},{5,7},{6,22},{7,5},{8,24},{9,11},... | collective-permute-start | bytes 884744 | tf_op jit(solution)/shard_map/ppermute | solution.py:995
  113.2 10.4 %last_blocks.1 = (bf16[256,768]{1,0:T(8,128)(2,1)}, bf16[256,768]{1,0:T(8,128)(2,1)}, bf16[2048,768]{1,0:T(8,128)(2,1)}) custom-call(s32[5]{0:T(128)} %stack.16.info, bf16[2,2048,128]{2,1,0:T(8,128)(2,1)} %get-tuple-element.220.refs_0_, bf16[2,2048,128]{2,1,0:T(8,128)(2,1)} %get-tuple-element.221.refs_1_, bf16[2,2048,128]{2,1,0:T(8,128)(2,1)} %get-tuple-element.222.refs_2_, ...), custom_call_target="tpu_custom_call" | custom-call | flops 5000000000 | bytes 15486976 | tf_op jit(solution)/shard_map/last_blocks/pallas_call | solution.py:250
  123.9 1.9 %collective-permute-start.12 = (bf16[288,512]{1,0:T(8,128)(2,1)S(1)}, bf16[288,512]{1,0:T(8,128)(2,1)S(1)}, u32[]{:S(2)}, u32[]{:S(2)}) collective-permute-start(bf16[288,512]{1,0:T(8,128)(2,1)S(1)} %add_convert_fusion.4), channel_id=1, source_target_pairs={{0,2},{1,5},{2,0},{3,7},{4,6},{5,1},{6,4},{7,3},{8,10},{9,13},{10,... | collective-permute-start | bytes 884744 | tf_op jit(solution)/shard_map/ppermute | solution.py:995
  125.9 7.8 %back_rows.1 = (bf16[1024,512]{1,0:T(8,128)(2,1)}, bf16[1024,512]{1,0:T(8,128)(2,1)}, bf16[1024,128]{1,0:T(8,128)(2,1)}, bf16[1024,128]{1,0:T(8,128)(2,1)}) custom-call(s32[5]{0:T(128)} %stack.16.info, bf16[2048,768]{1,0:T(8,128)(2,1)} %get-tuple-element.242.packed_in, bf16[512,512]{1,0:T(8,128)(2,1)} %query_in.3, bf16[512,512]{1,0:T(8,128)(2,1)} %key_in.3, ...), custom_call_target="tpu_custom_call" | custom-call | flops 2000000000 | bytes 7077888 | tf_op jit(solution)/shard_map/back_rows/pallas_call | solution.py:250
  133.6 1.3 collective-permute-done.12
  135.7 2.7 %collective-permute-start.14 = (bf16[576,512]{1,0:T(8,128)(2,1)S(1)}, bf16[576,512]{1,0:T(8,128)(2,1)S(1)}, u32[]{:S(2)}, u32[]{:S(2)}) collective-permute-start(bf16[576,512]{1,0:T(8,128)(2,1)S(1)} %constant_dynamic-update-slice_fusion.3), channel_id=1, source_target_pairs={{0,4},{1,9},{2,6},{3,11},{4,0},{5,13},{6,2},{7,15},{8,12},{9,1},{1... | collective-permute-start | bytes 1769480 | tf_op jit(solution)/shard_map/ppermute | solution.py:995
  138.9 9.6 %collective-permute-done.13 = bf16[128,768]{1,0:T(8,128)(2,1)} collective-permute-done((bf16[128,768]{1,0:T(8,128)(2,1)}, bf16[128,768]{1,0:T(8,128)(2,1)}, u32[]{:S(2)}, u32[]{:S(2)}) %collective-permute-start.13) | collective-permute-done | bytes 196640 | tf_op jit(solution)/shard_map/ppermute | solution.py:995
  150.2 2.0 %collective-permute-start.18 = (bf16[432,512]{1,0:T(8,128)(2,1)S(1)}, bf16[432,512]{1,0:T(8,128)(2,1)}, u32[]{:S(2)}, u32[]{:S(2)}) collective-permute-start(bf16[432,512]{1,0:T(8,128)(2,1)S(1)} %pad_maximum_fusion.7), channel_id=1, source_target_pairs={{0,2},{1,5},{2,0},{3,7},{4,6},{5,1},{6,4},{7,3},{8,10},{9,13},{10,... | collective-permute-start | bytes 1327112 | tf_op jit(solution)/shard_map/ppermute | solution.py:995
  152.5 5.8 %close_rows.1 = (bf16[1024,512]{1,0:T(8,128)(2,1)}, bf16[1024,256]{1,0:T(8,128)(2,1)}) custom-call(s32[5]{0:T(128)} %stack.16.info, bf16[1024,512]{1,0:T(8,128)(2,1)} %tokens_in.3, f32[1024,512]{1,0:T(8,128)} %get-tuple-element.261.after_grad_in, bf16[1024,512]{1,0:T(8,128)(2,1)} %get-tuple-element.262.back_own_in, bf16[1024,512]{1,0:T(8,128)(2,1)} %copy-done.2, ...), custom_call_target="tpu_custom_call" | custom-call | flops 100000000 | bytes 7342080 | tf_op jit(solution)/shard_map/close_rows/pallas_call | solution.py:250
  159.7 2.0 %collective-permute-start.20 = (bf16[432,512]{1,0:T(8,128)(2,1)S(1)}, bf16[432,512]{1,0:T(8,128)(2,1)S(1)}, u32[]{:S(2)}, u32[]{:S(2)}) collective-permute-start(bf16[432,512]{1,0:T(8,128)(2,1)S(1)} %slice.13), channel_id=1, source_target_pairs={{0,2},{1,5},{2,0},{3,7},{4,6},{5,1},{6,4},{7,3},{8,10},{9,13},{10,... | collective-permute-start | bytes 1327112 | tf_op jit(solution)/shard_map/ppermute | solution.py:995
  161.7 1.4 collective-permute-start.19
  165.0 2.6 %collective-permute-done.19 = bf16[64,768]{1,0:T(8,128)(2,1)S(1)} collective-permute-done((bf16[64,768]{1,0:T(8,128)(2,1)S(1)}, bf16[64,768]{1,0:T(8,128)(2,1)S(1)}, u32[]{:S(2)}, u32[]{:S(2)}) %collective-permute-start.19) | collective-permute-done | bytes 98336 | tf_op jit(solution)/shard_map/ppermute | solution.py:995
  168.6 1.8 collective-permute-start.21
  170.7 3.0 %unpack_half.1 = (f32[2048,512]{1,0:T(8,128)}, f32[512,2048]{1,0:T(8,128)}, f32[512,512]{1,0:T(8,128)}) custom-call(s32[5]{0:T(128)S(1)} %copy-done, bf16[2304,512]{1,0:T(8,128)(2,1)S(1)} %constant_dynamic-update-slice_fusion.refs_0_), custom_call_target="tpu_custom_call" | custom-call | flops 100000000 | bytes 11796480 | tf_op jit(solution)/shard_map/unpack_half/pallas_call | solution.py:250
  173.8 1.2 collective-permute-done.22
  175.1 1.9 %collective-permute-start.24 = (bf16[128,768]{1,0:T(8,128)(2,1)S(1)}, bf16[128,768]{1,0:T(8,128)(2,1)S(1)}, u32[]{:S(2)}, u32[]{:S(2)}) collective-permute-start(bf16[128,768]{1,0:T(8,128)(2,1)S(1)} %constant_dynamic-update-slice_fusion.5), channel_id=1, source_target_pairs={{0,4},{1,3},{2,6},{3,1},{4,0},{5,7},{6,2},{7,5},{8,12},{9,11},{10,... | collective-permute-start | bytes 589832 | tf_op jit(solution)/shard_map/ppermute | solution.py:995
  177.9 3.0 %unpack_late.1 = (f32[2048,512]{1,0:T(8,128)}, f32[512,2048]{1,0:T(8,128)}, f32[512,512]{1,0:T(8,128)}) custom-call(s32[5]{0:T(128)S(1)} %copy-done, bf16[2304,512]{1,0:T(8,128)(2,1)S(1)} %collective-permute-done.23.refs_0_, f32[2048,512]{1,0:T(8,128)} %get-tuple-element.292.refs_1_, ...), custom_call_target="tpu_custom_call", output_to_operand_aliasing={{0}: (2, {}), {1}: (3, {}), {2}: (4, {})} | custom-call | flops 100000000 | bytes 21233664 | tf_op jit(solution)/shard_map/unpack_late/pallas_call | solution.py:250
  182.8 4.7 %collective-permute-done.26 = bf16[128,768]{1,0:T(8,128)(2,1)S(1)} collective-permute-done((bf16[128,768]{1,0:T(8,128)(2,1)S(1)}, bf16[128,768]{1,0:T(8,128)(2,1)S(1)}, u32[]{:S(2)}, u32[]{:S(2)}) %collective-permute-start.26) | collective-permute-done | bytes 196640 | tf_op jit(solution)/shard_map/ppermute | solution.py:995
  187.8 1.5 collective-permute-done.28
  189.3 2.3 %split_projection.1 = (f32[512,512]{1,0:T(8,128)}, f32[512,512]{1,0:T(8,128)}, f32[512,256]{1,0:T(8,128)}, f32[1,512]{1,0:T(1,128)}, f32[1,512]{1,0:T(1,128)}, /...) custom-call(s32[5]{0:T(128)S(1)} %copy-done, ...), custom_call_target="tpu_custom_call" | custom-call | flops 100000000 | bytes 4210688 | tf_op jit(solution)/shard_map/split_projection/pallas_call | solution.py:250
  (93 shorter events, 19.2 us)
Async XLA Ops:
  0.6 3.8 %collective-permute-start = (bf16[1024,512]{1,0:T(8,128)(2,1)}, bf16[1024,512]{1,0:T(8,128)(2,1)S(1)}, u32[]{:S(2)}, u32[]{:S(2)}) collective-permute-start(bf16[1024,512]{1,0:T(8,128)(2,1)} %tokens_in.3), channel_id=1, source_target_pairs={{0,1},{1,0},{2,3},{3,2},{4,5},{5,4},{6,7},{7,6},{8,9},{9,8},{10,11... | collective-permute-start | bytes 3145736 | tf_op jit(solution)/shard_map/ppermute | solution.py:949
  1.2 3.2 %collective-permute-start.1 = (bf16[1024,256]{1,0:T(8,128)(2,1)}, bf16[1024,256]{1,0:T(8,128)(2,1)S(1)}, u32[]{:S(2)}, u32[]{:S(2)}) collective-permute-start(bf16[1024,256]{1,0:T(8,128)(2,1)} %skip_own_in.1), channel_id=1, source_target_pairs={{0,1},{1,0},{2,3},{3,2},{4,5},{5,4},{6,7},{7,6},{8,9},{9,8},{10,11... | collective-permute-start | bytes 1572872 | tf_op jit(solution)/shard_map/ppermute | solution.py:949
  27.7 2.2 %collective-permute-start.2 = (bf16[1024,256]{1,0:T(8,128)(2,1)}, bf16[1024,256]{1,0:T(8,128)(2,1)S(1)}, u32[]{:S(2)}, u32[]{:S(2)}) collective-permute-start(bf16[1024,256]{1,0:T(8,128)(2,1)} %get-tuple-element.166), channel_id=1, source_target_pairs={{0,1},{1,0},{2,3},{3,2},{4,5},{5,4},{6,7},{7,6},{8,9},{9,8},{10,11... | collective-permute-start | bytes 1572872 | tf_op jit(solution)/shard_map/ppermute | solution.py:949
  56.4 2.2 %collective-permute-start.3 = (bf16[1024,256]{1,0:T(8,128)(2,1)}, bf16[1024,256]{1,0:T(8,128)(2,1)S(1)}, u32[]{:S(2)}, u32[]{:S(2)}) collective-permute-start(bf16[1024,256]{1,0:T(8,128)(2,1)} %get-tuple-element.172), channel_id=1, source_target_pairs={{0,1},{1,0},{2,3},{3,2},{4,5},{5,4},{6,7},{7,6},{8,9},{9,8},{10,11... | collective-permute-start | bytes 1572872 | tf_op jit(solution)/shard_map/ppermute | solution.py:949
  58.5 5.4 %collective-permute-start.4 = (bf16[1152,512]{1,0:T(8,128)(2,1)}, bf16[1152,512]{1,0:T(8,128)(2,1)}, u32[]{:S(2)}, u32[]{:S(2)}) collective-permute-start(bf16[1152,512]{1,0:T(8,128)(2,1)} %get-tuple-element.177), channel_id=1, source_target_pairs={{0,1},{1,0},{2,3},{3,2},{4,5},{5,4},{6,7},{7,6},{8,9},{9,8},{10,11... | collective-permute-start | bytes 3538952 | tf_op jit(solution)/shard_map/ppermute | solution.py:949
  58.9 24.6 %collective-permute-start.6 = (bf16[1152,512]{1,0:T(8,128)(2,1)}, bf16[1152,512]{1,0:T(8,128)(2,1)S(1)}, u32[]{:S(2)}, u32[]{:S(2)}) collective-permute-start(bf16[1152,512]{1,0:T(8,128)(2,1)} %get-tuple-element.192), channel_id=1, source_target_pairs={{0,1},{1,0},{2,3},{3,2},{4,5},{5,4},{6,7},{7,6},{8,9},{9,8},{10,11... | collective-permute-start | bytes 3538952 | tf_op jit(solution)/shard_map/ppermute | solution.py:949
  65.9 17.5 %collective-permute-start.5 = (bf16[1152,512]{1,0:T(8,128)(2,1)S(1)}, bf16[1152,512]{1,0:T(8,128)(2,1)}, u32[]{:S(2)}, u32[]{:S(2)}) collective-permute-start(bf16[1152,512]{1,0:T(8,128)(2,1)S(1)} %add_convert_fusion.1), channel_id=1, source_target_pairs={{0,2},{1,5},{2,0},{3,7},{4,6},{5,1},{6,4},{7,3},{8,10},{9,13},{10,... | collective-permute-start | bytes 3538952 | tf_op jit(solution)/shard_map/ppermute | solution.py:995
  67.0 16.5 %copy-start.1 = (bf16[1152,512]{1,0:T(8,128)(2,1)S(1)}, bf16[1152,512]{1,0:T(8,128)(2,1)}, u32[]{:S(2)}) copy-start(bf16[1152,512]{1,0:T(8,128)(2,1)} %get-tuple-element.193) | copy-start | bytes 3538948
  85.0 14.4 %collective-permute-start.7 = (bf16[576,512]{1,0:T(8,128)(2,1)S(1)}, bf16[576,512]{1,0:T(8,128)(2,1)S(1)}, u32[]{:S(2)}, u32[]{:S(2)}) collective-permute-start(bf16[576,512]{1,0:T(8,128)(2,1)S(1)} %add_convert_fusion.3), channel_id=1, source_target_pairs={{0,4},{1,9},{2,6},{3,11},{4,0},{5,13},{6,2},{7,15},{8,12},{9,1},{1... | collective-permute-start | bytes 1769480 | tf_op jit(solution)/shard_map/ppermute | solution.py:995
  100.8 9.9 %collective-permute-start.8 = (bf16[288,512]{1,0:T(8,128)(2,1)S(1)}, bf16[288,512]{1,0:T(8,128)(2,1)S(1)}, u32[]{:S(2)}, u32[]{:S(2)}) collective-permute-start(bf16[288,512]{1,0:T(8,128)(2,1)S(1)} %add_convert_fusion.7), channel_id=1, source_target_pairs={{0,8},{1,17},{2,10},{3,19},{4,12},{5,21},{6,14},{7,23},{8,0},{9,25... | collective-permute-start | bytes 884744 | tf_op jit(solution)/shard_map/ppermute | solution.py:995
  110.9 12.7 %collective-permute-start.9 = (bf16[288,512]{1,0:T(8,128)(2,1)S(1)}, bf16[288,512]{1,0:T(8,128)(2,1)S(1)}, u32[]{:S(2)}, u32[]{:S(2)}) collective-permute-start(bf16[288,512]{1,0:T(8,128)(2,1)S(1)} %add_convert_fusion.5), channel_id=1, source_target_pairs={{0,16},{1,3},{2,18},{3,1},{4,20},{5,7},{6,22},{7,5},{8,24},{9,11},... | collective-permute-start | bytes 884744 | tf_op jit(solution)/shard_map/ppermute | solution.py:995
  123.7 11.2 %collective-permute-start.10 = (bf16[256,768]{1,0:T(8,128)(2,1)}, bf16[256,768]{1,0:T(8,128)(2,1)S(1)}, u32[]{:S(2)}, u32[]{:S(2)}) collective-permute-start(bf16[256,768]{1,0:T(8,128)(2,1)} %get-tuple-element.239), channel_id=1, source_target_pairs={{0,2},{1,5},{2,0},{3,7},{4,6},{5,1},{6,4},{7,3},{8,10},{9,13},{10,... | collective-permute-start | bytes 1179656 | tf_op jit(solution)/shard_map/ppermute | solution.py:995
  123.8 9.8 %collective-permute-start.11 = (bf16[288,512]{1,0:T(8,128)(2,1)S(1)}, bf16[288,512]{1,0:T(8,128)(2,1)S(1)}, u32[]{:S(2)}, u32[]{:S(2)}) collective-permute-start(bf16[288,512]{1,0:T(8,128)(2,1)S(1)} %add_convert_fusion.4), channel_id=1, source_target_pairs={{0,8},{1,17},{2,10},{3,19},{4,12},{5,21},{6,14},{7,23},{8,0},{9,25... | collective-permute-start | bytes 884744 | tf_op jit(solution)/shard_map/ppermute | solution.py:995
  123.9 11.0 %collective-permute-start.12 = (bf16[288,512]{1,0:T(8,128)(2,1)S(1)}, bf16[288,512]{1,0:T(8,128)(2,1)S(1)}, u32[]{:S(2)}, u32[]{:S(2)}) collective-permute-start(bf16[288,512]{1,0:T(8,128)(2,1)S(1)} %add_convert_fusion.4), channel_id=1, source_target_pairs={{0,2},{1,5},{2,0},{3,7},{4,6},{5,1},{6,4},{7,3},{8,10},{9,13},{10,... | collective-permute-start | bytes 884744 | tf_op jit(solution)/shard_map/ppermute | solution.py:995
  125.8 9.1 %copy-start.4 = (bf16[256,768]{1,0:T(8,128)(2,1)S(1)}, bf16[256,768]{1,0:T(8,128)(2,1)}, u32[]{:S(2)}) copy-start(bf16[256,768]{1,0:T(8,128)(2,1)} %get-tuple-element.232) | copy-start | bytes 1179652
  135.7 12.7 %collective-permute-start.15 = (bf16[1024,512]{1,0:T(8,128)(2,1)}, bf16[1024,512]{1,0:T(8,128)(2,1)S(1)}, u32[]{:S(2)}, u32[]{:S(2)}) collective-permute-start(bf16[1024,512]{1,0:T(8,128)(2,1)} %get-tuple-element.253), channel_id=1, source_target_pairs={{0,1},{1,0},{2,3},{3,2},{4,5},{5,4},{6,7},{7,6},{8,9},{9,8},{10,11... | collective-permute-start | bytes 3145736 | tf_op jit(solution)/shard_map/ppermute | solution.py:949
  135.7 12.7 %collective-permute-start.14 = (bf16[576,512]{1,0:T(8,128)(2,1)S(1)}, bf16[576,512]{1,0:T(8,128)(2,1)S(1)}, u32[]{:S(2)}, u32[]{:S(2)}) collective-permute-start(bf16[576,512]{1,0:T(8,128)(2,1)S(1)} %constant_dynamic-update-slice_fusion.3), channel_id=1, source_target_pairs={{0,4},{1,9},{2,6},{3,11},{4,0},{5,13},{6,2},{7,15},{8,12},{9,1},{1... | collective-permute-start | bytes 1769480 | tf_op jit(solution)/shard_map/ppermute | solution.py:995
  138.4 10.1 %collective-permute-start.16 = (bf16[1024,128]{1,0:T(8,128)(2,1)}, bf16[1024,128]{1,0:T(8,128)(2,1)S(1)}, u32[]{:S(2)}, u32[]{:S(2)}) collective-permute-start(bf16[1024,128]{1,0:T(8,128)(2,1)} %get-tuple-element.254), channel_id=1, source_target_pairs={{0,1},{1,0},{2,3},{3,2},{4,5},{5,4},{6,7},{7,6},{8,9},{9,8},{10,11... | collective-permute-start | bytes 786440 | tf_op jit(solution)/shard_map/ppermute | solution.py:949
  138.4 10.1 %collective-permute-start.13 = (bf16[128,768]{1,0:T(8,128)(2,1)}, bf16[128,768]{1,0:T(8,128)(2,1)}, u32[]{:S(2)}, u32[]{:S(2)}) collective-permute-start(bf16[128,768]{1,0:T(8,128)(2,1)} %get-tuple-element.251), channel_id=1, source_target_pairs={{0,4},{1,3},{2,6},{3,1},{4,0},{5,7},{6,2},{7,5},{8,12},{9,11},{10,... | collective-permute-start | bytes 589832 | tf_op jit(solution)/shard_map/ppermute | solution.py:995
  149.2 3.2 %copy-start.2 = (bf16[1024,512]{1,0:T(8,128)(2,1)}, bf16[1024,512]{1,0:T(8,128)(2,1)S(1)}, u32[]{:S(2)}) copy-start(bf16[1024,512]{1,0:T(8,128)(2,1)S(1)} %collective-permute-done.15.back_other_in) | copy-start | bytes 3145732
  150.2 8.5 %collective-permute-start.18 = (bf16[432,512]{1,0:T(8,128)(2,1)S(1)}, bf16[432,512]{1,0:T(8,128)(2,1)}, u32[]{:S(2)}, u32[]{:S(2)}) collective-permute-start(bf16[432,512]{1,0:T(8,128)(2,1)S(1)} %pad_maximum_fusion.7), channel_id=1, source_target_pairs={{0,2},{1,5},{2,0},{3,7},{4,6},{5,1},{6,4},{7,3},{8,10},{9,13},{10,... | collective-permute-start | bytes 1327112 | tf_op jit(solution)/shard_map/ppermute | solution.py:995
  152.4 5.9 %collective-permute-start.17 = (bf16[64,768]{1,0:T(8,128)(2,1)S(1)}, bf16[64,768]{1,0:T(8,128)(2,1)S(1)}, u32[]{:S(2)}, u32[]{:S(2)}) collective-permute-start(bf16[64,768]{1,0:T(8,128)(2,1)S(1)} %add_convert_fusion.13), channel_id=1, source_target_pairs={{0,8},{1,9},{2,10},{3,11},{4,12},{5,13},{6,14},{7,15},{8,0},{9,1},... | collective-permute-start | bytes 294920 | tf_op jit(solution)/shard_map/ppermute | solution.py:995
  159.7 8.4 %collective-permute-start.20 = (bf16[432,512]{1,0:T(8,128)(2,1)S(1)}, bf16[432,512]{1,0:T(8,128)(2,1)S(1)}, u32[]{:S(2)}, u32[]{:S(2)}) collective-permute-start(bf16[432,512]{1,0:T(8,128)(2,1)S(1)} %slice.13), channel_id=1, source_target_pairs={{0,2},{1,5},{2,0},{3,7},{4,6},{5,1},{6,4},{7,3},{8,10},{9,13},{10,... | collective-permute-start | bytes 1327112 | tf_op jit(solution)/shard_map/ppermute | solution.py:995
  161.7 6.0 %collective-permute-start.19 = (bf16[64,768]{1,0:T(8,128)(2,1)S(1)}, bf16[64,768]{1,0:T(8,128)(2,1)S(1)}, u32[]{:S(2)}, u32[]{:S(2)}) collective-permute-start(bf16[64,768]{1,0:T(8,128)(2,1)S(1)} %add_convert_fusion.11), channel_id=1, source_target_pairs={{0,16},{1,17},{2,18},{3,19},{4,20},{5,21},{6,22},{7,23},{8,24},{9,... | collective-permute-start | bytes 294920 | tf_op jit(solution)/shard_map/ppermute | solution.py:995
  168.5 6.5 %collective-permute-start.23 = (bf16[2304,512]{1,0:T(8,128)(2,1)S(1)}, bf16[2304,512]{1,0:T(8,128)(2,1)S(1)}, u32[]{:S(2)}, u32[]{:S(2)}) collective-permute-start(bf16[2304,512]{1,0:T(8,128)(2,1)S(1)} %constant_dynamic-update-slice_fusion.refs_0_), channel_id=1, source_target_pairs={{0,1},{1,0},{2,3},{3,2},{4,5},{5,4},{6,7},{7,6},{8,9},{9,8},{10,11... | collective-permute-start | bytes 7077896 | tf_op jit(solution)/shard_map/ppermute | solution.py:949
  168.6 5.2 %collective-permute-start.21 = (bf16[64,768]{1,0:T(8,128)(2,1)S(1)}, bf16[64,768]{1,0:T(8,128)(2,1)S(1)}, u32[]{:S(2)}, u32[]{:S(2)}) collective-permute-start(bf16[64,768]{1,0:T(8,128)(2,1)S(1)} %add_convert_fusion.10), channel_id=1, source_target_pairs={{0,8},{1,9},{2,10},{3,11},{4,12},{5,13},{6,14},{7,15},{8,0},{9,1},... | collective-permute-start | bytes 294920 | tf_op jit(solution)/shard_map/ppermute | solution.py:995
  170.4 4.6 %collective-permute-start.22 = (bf16[64,768]{1,0:T(8,128)(2,1)S(1)}, bf16[64,768]{1,0:T(8,128)(2,1)S(1)}, u32[]{:S(2)}, u32[]{:S(2)}) collective-permute-start(bf16[64,768]{1,0:T(8,128)(2,1)S(1)} %add_convert_fusion.10), channel_id=1, source_target_pairs={{0,2},{1,5},{2,0},{3,7},{4,6},{5,1},{6,4},{7,3},{8,10},{9,13},{10,... | collective-permute-start | bytes 294920 | tf_op jit(solution)/shard_map/ppermute | solution.py:995
  175.1 6.6 %collective-permute-start.24 = (bf16[128,768]{1,0:T(8,128)(2,1)S(1)}, bf16[128,768]{1,0:T(8,128)(2,1)S(1)}, u32[]{:S(2)}, u32[]{:S(2)}) collective-permute-start(bf16[128,768]{1,0:T(8,128)(2,1)S(1)} %constant_dynamic-update-slice_fusion.5), channel_id=1, source_target_pairs={{0,4},{1,3},{2,6},{3,1},{4,0},{5,7},{6,2},{7,5},{8,12},{9,11},{10,... | collective-permute-start | bytes 589832 | tf_op jit(solution)/shard_map/ppermute | solution.py:995
  177.0 4.6 %collective-permute-start.25 = (bf16[64,768]{1,0:T(8,128)(2,1)S(1)}, bf16[64,768]{1,0:T(8,128)(2,1)S(1)}, u32[]{:S(2)}, u32[]{:S(2)}) collective-permute-start(bf16[64,768]{1,0:T(8,128)(2,1)S(1)} %collective-permute-done.21), channel_id=1, source_target_pairs={{0,2},{1,5},{2,0},{3,7},{4,6},{5,1},{6,4},{7,3},{8,10},{9,13},{10,... | collective-permute-start | bytes 294920 | tf_op jit(solution)/shard_map/ppermute | solution.py:995
  181.6 5.8 %collective-permute-start.27 = (bf16[256,768]{1,0:T(8,128)(2,1)S(1)}, bf16[256,768]{1,0:T(8,128)(2,1)S(1)}, u32[]{:S(2)}, u32[]{:S(2)}) collective-permute-start(bf16[256,768]{1,0:T(8,128)(2,1)S(1)} %constant_dynamic-update-slice_fusion.2), channel_id=1, source_target_pairs={{0,1},{1,0},{2,3},{3,2},{4,5},{5,4},{6,7},{7,6},{8,9},{9,8},{10,11... | collective-permute-start | bytes 1179656 | tf_op jit(solution)/shard_map/ppermute | solution.py:949
  181.7 5.7 %collective-permute-start.26 = (bf16[128,768]{1,0:T(8,128)(2,1)S(1)}, bf16[128,768]{1,0:T(8,128)(2,1)S(1)}, u32[]{:S(2)}, u32[]{:S(2)}) collective-permute-start(bf16[128,768]{1,0:T(8,128)(2,1)S(1)} %collective-permute-done.24), channel_id=1, source_target_pairs={{0,2},{1,5},{2,0},{3,7},{4,6},{5,1},{6,4},{7,3},{8,10},{9,13},{10,... | collective-permute-start | bytes 589832 | tf_op jit(solution)/shard_map/ppermute | solution.py:995
  187.5 1.8 collective-permute-start.28
  (6 other events, 6.5 us)
where the time goes:
time: 195 us; the launch traced here: 192 us
  Pallas kernels  124 us (64%)
  waiting for transfers between devices  28.2 us (14%)
  starting transfers between devices  23.4 us (12%)
  other arithmetic  8.54 us (4%)
  local copies, waits for them, and re-layouts  5.72 us (3%)
  between operations  2.26 us (1%)
    pallas_call x12, Pallas kernels, run_kernel(): pl.pallas_call(kernel, in_specs=[smem] * len(scalars) + [large] * len(arg...  124 us
    ppermute x18, waiting for transfers between devices, swap(): return lax.ppermute(array, ('seq', 'head'), pairs)  21.3 us
    ppermute x18, starting transfers between devices, swap(): return lax.ppermute(array, ('seq', 'head'), pairs)  21.2 us
    convert_element_type x11, other arithmetic, add_low(): return (a.astype(F32) + b.astype(F32)).astype(BF16)  7.76 us
    ppermute x11, waiting for transfers between devices, swap_cores(): return lax.ppermute(array, 'head', [(0, 1), (1, 0)])  6.97 us
  transfers between devices with their start and end apart: 29, of which 14 were waited for; matrix products, arithmetic and copies ran while one was open for 3% of the time, Pallas kernels for 38%

commit v1 on v0

--- a/solution.py
+++ b/solution.py
@@ -14,7 +14,7 @@
 MASKED = -1e30
 EPS = 1e-05
 MIB = 1 << 20
-VMEM_MIB, WHOLE_MIB = 56, 62
+VMEM_MIB, WHOLE_MIB = 56, 58
 
 
 def nn(a, b):
@@ -1047,10 +1047,13 @@
         piece = join(self.mine, self.coming, self.which(self.next)) if self.fitting else self.added()
         far, mid, near = self.trail
         rows = piece.shape[0]
-        came_near, got_own = yield [(self.via(near), piece), (self.via(far), piece)]
+        if small:
+            (came_near,) = yield [(self.via(near), piece)]
+        else:
+            came_near, got_own = yield [(self.via(near), piece), (self.via(far), piece)]
         both = join(piece, came_near, self.which(near))
         if small:
-            came_mid, got_near = yield [(self.via(mid), both), (self.via(far), came_near)]
+            came_mid, got = yield [(self.via(mid), both), (self.via(far), both)]
             self.mine = join(both, came_mid, self.which(mid))
             got_mid, other_mine = yield [(self.via(far), came_mid), (swap_cores, self.mine)]
         else:
@@ -1058,9 +1061,10 @@
             cut = rows // 32 * 16
             (first,) = yield [(self.via(far), jnp.concatenate([came_near, came_mid[:cut]], axis=0))]
             (second,) = yield [(self.via(far), came_mid[cut:])]
-            got_near, got_mid = first[:rows], jnp.concatenate([first[rows:], second], axis=0)
+            got = join(got_own, first[:rows], self.which(near))
+            got_mid = jnp.concatenate([first[rows:], second], axis=0)
             self.mine = join(both, came_mid, self.which(mid))
-        theirs = join(join(got_own, got_near, self.which(near)), got_mid, self.which(mid))
+        theirs = join(got, got_mid, self.which(mid))
         self.mine = join(self.mine, theirs, self.which(far))
         self.whole = True
         if small:
@@ -1072,7 +1076,7 @@
 
 ORDERS = ((0, 1, 2, 3), (1, 2, 3, 0))
 PROJECTION_ORDERS = ((0, 1, 2, 3), (1, 0, 2, 3))
-CUTS = (0, 2, 4, 6, 8)
+CUTS = (0, 2, 5, 8)
 
 
 def on_device(

time: 195 us -> 190 us (0.974)
  other arithmetic: 8.54 us -> 3.92 us
  waiting for transfers between devices: 28.2 us -> 32.2 us
  Pallas kernels: 124 us -> 121 us
    convert_element_type x11, other arithmetic: 7.76 us -> 3.16 us  [add_low(): return (a.astype(F32) + b.astype(F32)).astype(BF16)]
    ppermute x18 -> x17, waiting for transfers between devices: 21.3 us -> 25.2 us  [swap(): return lax.ppermute(array, ('seq', 'head'), pairs)]
    pallas_call x12 -> x11, Pallas kernels: 124 us -> 121 us  [run_kernel(): pl.pallas_call(kernel, in_specs=[smem] * len(scalars) + [large] * len(arg...]
    ppermute x18 -> x17, starting transfers between devices: 21.2 us -> 21.9 us  [swap(): return lax.ppermute(array, ('seq', 'head'), pairs)]
  transfers between devices with their start and end apart: 29 -> 28, of which waited for: 14 -> 13; matrix products, arithmetic and copies ran while one was open for 3% -> 1% of each run, Pallas kernels for 38% -> 38%
where the time goes in v1:
time: 190 us; the launch traced here: 187 us
  Pallas kernels  121 us (64%)
  waiting for transfers between devices  32.2 us (17%)
  starting transfers between devices  24.3 us (13%)
  local copies, waits for them, and re-layouts  4.03 us (2%)
  other arithmetic  3.92 us (2%)
  between operations  2.02 us (1%)
    pallas_call x11, Pallas kernels, run_kernel(): pl.pallas_call(kernel, in_specs=[smem] * len(scalars) + [large] * len(arg...  121 us
    ppermute x17, waiting for transfers between devices, swap(): return lax.ppermute(array, ('seq', 'head'), pairs)  25.2 us
    ppermute x17, starting transfers between devices, swap(): return lax.ppermute(array, ('seq', 'head'), pairs)  21.9 us
    ppermute x11, waiting for transfers between devices, swap_cores(): return lax.ppermute(array, 'head', [(0, 1), (1, 0)])  6.96 us
  transfers between devices with their start and end apart: 28, of which 13 were waited for; matrix products, arithmetic and copies ran while one was open for 1% of the time, Pallas kernels for 38%

profile of v1, /device:TPU:0, one launch (start us, length us, event | category | flops | bytes accessed | tf_op | source)
XLA Modules:
  0.0 187.1 jit_solution(13816375899962110291)
XLA Ops:
  2.5 1.9 %collective-permute-done.1.skip_other_in = bf16[1024,256]{1,0:T(8,128)(2,1)S(1)} collective-permute-done((bf16[1024,256]{1,0:T(8,128)(2,1)}, bf16[1024,256]{1,0:T(8,128)(2,1)S(1)}, u32[]{:S(2)}, u32[]{:S(2)}) %collective-permute-start.1) | collective-permute-done | bytes 524320 | tf_op jit(solution)/shard_map/ppermute | solution.py:949
  5.6 21.9 %forward_attention.1 = (bf16[1024,256]{1,0:T(8,128)(2,1)}, bf16[1024,256]{1,0:T(8,128)(2,1)}, bf16[2,2048,128]{2,1,0:T(8,128)(2,1)}, bf16[2,2048,128]{2,1,0:T(8,...) custom-call(s32[5]{0:T(128)} %stack.16.info, ...), custom_call_target="tpu_custom_call" | custom-call | flops 10000000000 | bytes 11931648 | tf_op jit(solution)/shard_map/forward_attention/pallas_call | solution.py:250
  27.9 1.7 collective-permute-done.2.mixed_other_in
  30.4 25.7 %row_part.1 = (bf16[1024,512]{1,0:T(8,128)(2,1)}, f32[1024,512]{1,0:T(8,128)}, bf16[1024,256]{1,0:T(8,128)(2,1)}, bf16[1024,256]{1,0:T(8,128)(2,1)}, bf16[1152,5...) custom-call(s32[5]{0:T(128)} %stack.16.info, ...), custom_call_target="tpu_custom_call" | custom-call | flops 15000000512 | bytes 16805888 | tf_op jit(solution)/shard_map/row_part/pallas_call | solution.py:250
  56.5 1.7 collective-permute-done.3.grad_other_in
  59.1 4.6 %arrange_rows.1 = (bf16[2,2048,128]{2,1,0:T(8,128)(2,1)}, f32[2,8,2048]{2,1,0:T(8,128)}) custom-call(s32[5]{0:T(128)} %stack.16.info, bf16[1024,256]{1,0:T(8,128)(2,1)} %get-tuple-element.159.grad_own_in, bf16[1024,256]{1,0:T(8,128)(2,1)} %copy-done.4, bf16[2,2048,128]{2,1,0:T(8,128)(2,1)} %get-tuple-element.163.mixed_in), custom_call_target="tpu_custom_call" | custom-call | flops 100000000 | bytes 3276800 | tf_op jit(solution)/shard_map/arrange_rows/pallas_call | solution.py:250
  64.1 1.1 collective-permute-start.5
  65.2 16.6 %blocks_0.1 = (f32[2,2048,128]{2,1,0:T(8,128)}, bf16[512,512]{1,0:T(8,128)(2,1)}) custom-call(s32[5]{0:T(128)} %stack.16.info, bf16[2,2048,128]{2,1,0:T(8,128)(2,1)} %get-tuple-element.196.refs_0_, bf16[2,2048,128]{2,1,0:T(8,128)(2,1)} %get-tuple-element.197.refs_1_, bf16[2,2048,128]{2,1,0:T(8,128)(2,1)} %get-tuple-element.198.refs_2_, ...), custom_call_target="tpu_custom_call" | custom-call | flops 5000000000 | bytes 7077888 | tf_op jit(solution)/shard_map/blocks_0/pallas_call | solution.py:250
  82.3 3.4 %collective-permute-start.7 = (bf16[576,512]{1,0:T(8,128)(2,1)S(1)}, bf16[576,512]{1,0:T(8,128)(2,1)S(1)}, u32[]{:S(2)}, u32[]{:S(2)}) collective-permute-start(bf16[576,512]{1,0:T(8,128)(2,1)S(1)} %add_convert_fusion.3), channel_id=1, source_target_pairs={{0,4},{1,9},{2,6},{3,11},{4,0},{5,13},{6,2},{7,15},{8,12},{9,1},{1... | collective-permute-start | bytes 1769480 | tf_op jit(solution)/shard_map/ppermute | solution.py:995
  85.8 16.8 %blocks_2.1 = (f32[2,2048,128]{2,1,0:T(8,128)}, bf16[768,512]{1,0:T(8,128)(2,1)}) custom-call(s32[5]{0:T(128)} %stack.16.info, bf16[2,2048,128]{2,1,0:T(8,128)(2,1)} %get-tuple-element.196.refs_0_, bf16[2,2048,128]{2,1,0:T(8,128)(2,1)} %get-tuple-element.197.refs_1_, ...), custom_call_target="tpu_custom_call", output_to_operand_aliasing={{0}: (7, {})} | custom-call | flops 5000000000 | bytes 9437184 | tf_op jit(solution)/shard_map/blocks_2/pallas_call | solution.py:250
  102.9 13.1 %last_blocks.1 = (bf16[256,768]{1,0:T(8,128)(2,1)}, bf16[256,768]{1,0:T(8,128)(2,1)}, bf16[2048,768]{1,0:T(8,128)(2,1)}) custom-call(s32[5]{0:T(128)} %stack.16.info, bf16[2,2048,128]{2,1,0:T(8,128)(2,1)} %get-tuple-element.196.refs_0_, bf16[2,2048,128]{2,1,0:T(8,128)(2,1)} %get-tuple-element.197.refs_1_, bf16[2,2048,128]{2,1,0:T(8,128)(2,1)} %get-tuple-element.198.refs_2_, ...), custom_call_target="tpu_custom_call" | custom-call | flops 5000000000 | bytes 15224832 | tf_op jit(solution)/shard_map/last_blocks/pallas_call | solution.py:250
  117.1 7.8 %back_rows.1 = (bf16[1024,512]{1,0:T(8,128)(2,1)}, bf16[1024,512]{1,0:T(8,128)(2,1)}, bf16[1024,128]{1,0:T(8,128)(2,1)}, bf16[1024,128]{1,0:T(8,128)(2,1)}) custom-call(s32[5]{0:T(128)} %stack.16.info, bf16[2048,768]{1,0:T(8,128)(2,1)} %get-tuple-element.217.packed_in, bf16[512,512]{1,0:T(8,128)(2,1)} %query_in.3, bf16[512,512]{1,0:T(8,128)(2,1)} %key_in.3, ...), custom_call_target="tpu_custom_call" | custom-call | flops 2000000000 | bytes 7077888 | tf_op jit(solution)/shard_map/back_rows/pallas_call | solution.py:250
  124.9 3.0 %collective-permute-done.10 = bf16[288,512]{1,0:T(8,128)(2,1)S(1)} collective-permute-done((bf16[288,512]{1,0:T(8,128)(2,1)S(1)}, bf16[288,512]{1,0:T(8,128)(2,1)S(1)}, u32[]{:S(2)}, u32[]{:S(2)}) %collective-permute-start.10) | collective-permute-done | bytes 294944 | tf_op jit(solution)/shard_map/ppermute | solution.py:995
  128.4 2.5 %collective-permute-start.13 = (bf16[288,512]{1,0:T(8,128)(2,1)S(1)}, bf16[288,512]{1,0:T(8,128)(2,1)S(1)}, u32[]{:S(2)}, u32[]{:S(2)}) collective-permute-start(bf16[288,512]{1,0:T(8,128)(2,1)S(1)} %add_convert_fusion.4), channel_id=1, source_target_pairs={{0,2},{1,5},{2,0},{3,7},{4,6},{5,1},{6,4},{7,3},{8,10},{9,13},{10,... | collective-permute-start | bytes 884744 | tf_op jit(solution)/shard_map/ppermute | solution.py:995
  130.9 2.6 %collective-permute-start.11 = (bf16[128,768]{1,0:T(8,128)(2,1)S(1)}, bf16[128,768]{1,0:T(8,128)(2,1)S(1)}, u32[]{:S(2)}, u32[]{:S(2)}) collective-permute-start(bf16[128,768]{1,0:T(8,128)(2,1)S(1)} %get-tuple-element.226), channel_id=1, source_target_pairs={{0,4},{1,3},{2,6},{3,1},{4,0},{5,7},{6,2},{7,5},{8,12},{9,11},{10,... | collective-permute-start | bytes 589832 | tf_op jit(solution)/shard_map/ppermute | solution.py:995
  133.5 4.2 %collective-permute-done.11 = bf16[128,768]{1,0:T(8,128)(2,1)S(1)} collective-permute-done((bf16[128,768]{1,0:T(8,128)(2,1)S(1)}, bf16[128,768]{1,0:T(8,128)(2,1)S(1)}, u32[]{:S(2)}, u32[]{:S(2)}) %collective-permute-start.11) | collective-permute-done | bytes 196640 | tf_op jit(solution)/shard_map/ppermute | solution.py:995
  138.7 1.8 collective-permute-start.17
  140.5 1.2 collective-permute-start.16
  141.7 5.8 %close_rows.1 = (bf16[1024,512]{1,0:T(8,128)(2,1)}, bf16[1024,256]{1,0:T(8,128)(2,1)}) custom-call(s32[5]{0:T(128)} %stack.16.info, bf16[1024,512]{1,0:T(8,128)(2,1)} %tokens_in.3, f32[1024,512]{1,0:T(8,128)} %get-tuple-element.237.after_grad_in, bf16[1024,512]{1,0:T(8,128)(2,1)} %get-tuple-element.238.back_own_in, bf16[1024,512]{1,0:T(8,128)(2,1)} %copy-done.3, ...), custom_call_target="tpu_custom_call" | custom-call | flops 100000000 | bytes 7342080 | tf_op jit(solution)/shard_map/close_rows/pallas_call | solution.py:250
  149.6 2.5 %collective-permute-start.19 = (bf16[432,512]{1,0:T(8,128)(2,1)S(1)}, bf16[432,512]{1,0:T(8,128)(2,1)S(1)}, u32[]{:S(2)}, u32[]{:S(2)}) collective-permute-start(bf16[432,512]{1,0:T(8,128)(2,1)S(1)} %pad_maximum_fusion.7), channel_id=1, source_target_pairs={{0,2},{1,5},{2,0},{3,7},{4,6},{5,1},{6,4},{7,3},{8,10},{9,13},{10,... | collective-permute-start | bytes 1327112 | tf_op jit(solution)/shard_map/ppermute | solution.py:995
  152.2 2.2 %collective-permute-start.18 = (bf16[64,768]{1,0:T(8,128)(2,1)S(1)}, bf16[64,768]{1,0:T(8,128)(2,1)S(1)}, u32[]{:S(2)}, u32[]{:S(2)}) collective-permute-start(bf16[64,768]{1,0:T(8,128)(2,1)S(1)} %add_convert_fusion.11), channel_id=1, source_target_pairs={{0,16},{1,17},{2,18},{3,19},{4,20},{5,21},{6,22},{7,23},{8,24},{9,... | collective-permute-start | bytes 294920 | tf_op jit(solution)/shard_map/ppermute | solution.py:995
  154.5 6.0 %collective-permute-done.18 = bf16[64,768]{1,0:T(8,128)(2,1)S(1)} collective-permute-done((bf16[64,768]{1,0:T(8,128)(2,1)S(1)}, bf16[64,768]{1,0:T(8,128)(2,1)S(1)}, u32[]{:S(2)}, u32[]{:S(2)}) %collective-permute-start.18) | collective-permute-done | bytes 98336 | tf_op jit(solution)/shard_map/ppermute | solution.py:995
  160.6 1.6 collective-permute-start.20
  162.3 3.2 %collective-permute-done.20 = bf16[64,768]{1,0:T(8,128)(2,1)S(1)} collective-permute-done((bf16[64,768]{1,0:T(8,128)(2,1)S(1)}, bf16[64,768]{1,0:T(8,128)(2,1)S(1)}, u32[]{:S(2)}, u32[]{:S(2)}) %collective-permute-start.20) | collective-permute-done | bytes 98336 | tf_op jit(solution)/shard_map/ppermute | solution.py:995
  165.5 3.4 %collective-permute-done.21 = bf16[432,512]{1,0:T(8,128)(2,1)S(1)} collective-permute-done((bf16[432,512]{1,0:T(8,128)(2,1)S(1)}, bf16[432,512]{1,0:T(8,128)(2,1)S(1)}, u32[]{:S(2)}, u32[]{:S(2)}) %collective-permute-start.21) | collective-permute-done | bytes 442400 | tf_op jit(solution)/shard_map/ppermute | solution.py:995
  170.0 1.7 collective-permute-start.23
  171.7 3.0 %unpack_half.1 = (f32[2048,512]{1,0:T(8,128)}, f32[512,2048]{1,0:T(8,128)}, f32[512,512]{1,0:T(8,128)}) custom-call(s32[5]{0:T(128)S(1)} %copy-done, bf16[2304,512]{1,0:T(8,128)(2,1)S(1)} %constant_dynamic-update-slice_fusion.2.refs_0_), custom_call_target="tpu_custom_call" | custom-call | flops 100000000 | bytes 11796480 | tf_op jit(solution)/shard_map/unpack_half/pallas_call | solution.py:250
  174.7 2.1 %collective-permute-done.22 = bf16[128,768]{1,0:T(8,128)(2,1)S(1)} collective-permute-done((bf16[128,768]{1,0:T(8,128)(2,1)S(1)}, bf16[128,768]{1,0:T(8,128)(2,1)S(1)}, u32[]{:S(2)}, u32[]{:S(2)}) %collective-permute-start.22) | collective-permute-done | bytes 196640 | tf_op jit(solution)/shard_map/ppermute | solution.py:995
  177.5 3.0 %unpack_late.1 = (f32[2048,512]{1,0:T(8,128)}, f32[512,2048]{1,0:T(8,128)}, f32[512,512]{1,0:T(8,128)}) custom-call(s32[5]{0:T(128)S(1)} %copy-done, bf16[2304,512]{1,0:T(8,128)(2,1)S(1)} %collective-permute-done.24.refs_0_, f32[2048,512]{1,0:T(8,128)} %get-tuple-element.273.refs_1_, ...), custom_call_target="tpu_custom_call", output_to_operand_aliasing={{0}: (2, {}), {1}: (3, {}), {2}: (4, {})} | custom-call | flops 100000000 | bytes 21233664 | tf_op jit(solution)/shard_map/unpack_late/pallas_call | solution.py:250
  180.6 2.1 %collective-permute-done.25 = bf16[128,768]{1,0:T(8,128)(2,1)S(1)} collective-permute-done((bf16[128,768]{1,0:T(8,128)(2,1)S(1)}, bf16[128,768]{1,0:T(8,128)(2,1)S(1)}, u32[]{:S(2)}, u32[]{:S(2)}) %collective-permute-start.25) | collective-permute-done | bytes 196640 | tf_op jit(solution)/shard_map/ppermute | solution.py:995
  183.0 1.5 collective-permute-done.27
  184.6 2.3 %split_projection.1 = (f32[512,512]{1,0:T(8,128)}, f32[512,512]{1,0:T(8,128)}, f32[512,256]{1,0:T(8,128)}, f32[1,512]{1,0:T(1,128)}, f32[1,512]{1,0:T(1,128)}, /...) custom-call(s32[5]{0:T(128)S(1)} %copy-done, ...), custom_call_target="tpu_custom_call" | custom-call | flops 100000000 | bytes 4210688 | tf_op jit(solution)/shard_map/split_projection/pallas_call | solution.py:250
  (92 shorter events, 12.8 us)
Async XLA Ops:
  0.6 3.8 %collective-permute-start = (bf16[1024,512]{1,0:T(8,128)(2,1)}, bf16[1024,512]{1,0:T(8,128)(2,1)S(1)}, u32[]{:S(2)}, u32[]{:S(2)}) collective-permute-start(bf16[1024,512]{1,0:T(8,128)(2,1)} %tokens_in.3), channel_id=1, source_target_pairs={{0,1},{1,0},{2,3},{3,2},{4,5},{5,4},{6,7},{7,6},{8,9},{9,8},{10,11... | collective-permute-start | bytes 3145736 | tf_op jit(solution)/shard_map/ppermute | solution.py:949
  1.2 3.2 %collective-permute-start.1 = (bf16[1024,256]{1,0:T(8,128)(2,1)}, bf16[1024,256]{1,0:T(8,128)(2,1)S(1)}, u32[]{:S(2)}, u32[]{:S(2)}) collective-permute-start(bf16[1024,256]{1,0:T(8,128)(2,1)} %skip_own_in.1), channel_id=1, source_target_pairs={{0,1},{1,0},{2,3},{3,2},{4,5},{5,4},{6,7},{7,6},{8,9},{9,8},{10,11... | collective-permute-start | bytes 1572872 | tf_op jit(solution)/shard_map/ppermute | solution.py:949
  27.4 2.2 %collective-permute-start.2 = (bf16[1024,256]{1,0:T(8,128)(2,1)}, bf16[1024,256]{1,0:T(8,128)(2,1)S(1)}, u32[]{:S(2)}, u32[]{:S(2)}) collective-permute-start(bf16[1024,256]{1,0:T(8,128)(2,1)} %get-tuple-element.154), channel_id=1, source_target_pairs={{0,1},{1,0},{2,3},{3,2},{4,5},{5,4},{6,7},{7,6},{8,9},{9,8},{10,11... | collective-permute-start | bytes 1572872 | tf_op jit(solution)/shard_map/ppermute | solution.py:949
  56.1 7.6 %copy-start.2 = (bf16[1152,512]{1,0:T(8,128)(2,1)S(1)}, bf16[1152,512]{1,0:T(8,128)(2,1)}, u32[]{:S(2)}) copy-start(bf16[1152,512]{1,0:T(8,128)(2,1)} %get-tuple-element.169) | copy-start | bytes 3538948
  56.1 2.2 %collective-permute-start.3 = (bf16[1024,256]{1,0:T(8,128)(2,1)}, bf16[1024,256]{1,0:T(8,128)(2,1)S(1)}, u32[]{:S(2)}, u32[]{:S(2)}) collective-permute-start(bf16[1024,256]{1,0:T(8,128)(2,1)} %get-tuple-element.160), channel_id=1, source_target_pairs={{0,1},{1,0},{2,3},{3,2},{4,5},{5,4},{6,7},{7,6},{8,9},{9,8},{10,11... | collective-permute-start | bytes 1572872 | tf_op jit(solution)/shard_map/ppermute | solution.py:949
  58.3 5.4 %collective-permute-start.4 = (bf16[1152,512]{1,0:T(8,128)(2,1)}, bf16[1152,512]{1,0:T(8,128)(2,1)S(1)}, u32[]{:S(2)}, u32[]{:S(2)}) collective-permute-start(bf16[1152,512]{1,0:T(8,128)(2,1)} %get-tuple-element.165), channel_id=1, source_target_pairs={{0,1},{1,0},{2,3},{3,2},{4,5},{5,4},{6,7},{7,6},{8,9},{9,8},{10,11... | collective-permute-start | bytes 3538952 | tf_op jit(solution)/shard_map/ppermute | solution.py:949
  58.7 23.1 %collective-permute-start.6 = (bf16[1152,512]{1,0:T(8,128)(2,1)}, bf16[1152,512]{1,0:T(8,128)(2,1)S(1)}, u32[]{:S(2)}, u32[]{:S(2)}) collective-permute-start(bf16[1152,512]{1,0:T(8,128)(2,1)} %get-tuple-element.180), channel_id=1, source_target_pairs={{0,1},{1,0},{2,3},{3,2},{4,5},{5,4},{6,7},{7,6},{8,9},{9,8},{10,11... | collective-permute-start | bytes 3538952 | tf_op jit(solution)/shard_map/ppermute | solution.py:949
  64.1 17.7 %collective-permute-start.5 = (bf16[1152,512]{1,0:T(8,128)(2,1)S(1)}, bf16[1152,512]{1,0:T(8,128)(2,1)S(1)}, u32[]{:S(2)}, u32[]{:S(2)}) collective-permute-start(bf16[1152,512]{1,0:T(8,128)(2,1)S(1)} %add_convert_fusion.1), channel_id=1, source_target_pairs={{0,2},{1,5},{2,0},{3,7},{4,6},{5,1},{6,4},{7,3},{8,10},{9,13},{10,... | collective-permute-start | bytes 3538952 | tf_op jit(solution)/shard_map/ppermute | solution.py:995
  65.2 16.7 %copy-start.1 = (bf16[1152,512]{1,0:T(8,128)(2,1)S(1)}, bf16[1152,512]{1,0:T(8,128)(2,1)}, u32[]{:S(2)}) copy-start(bf16[1152,512]{1,0:T(8,128)(2,1)} %get-tuple-element.181) | copy-start | bytes 3538948
  82.3 20.2 %collective-permute-start.7 = (bf16[576,512]{1,0:T(8,128)(2,1)S(1)}, bf16[576,512]{1,0:T(8,128)(2,1)S(1)}, u32[]{:S(2)}, u32[]{:S(2)}) collective-permute-start(bf16[576,512]{1,0:T(8,128)(2,1)S(1)} %add_convert_fusion.3), channel_id=1, source_target_pairs={{0,4},{1,9},{2,6},{3,11},{4,0},{5,13},{6,2},{7,15},{8,12},{9,1},{1... | collective-permute-start | bytes 1769480 | tf_op jit(solution)/shard_map/ppermute | solution.py:995
  102.8 13.2 %collective-permute-start.8 = (bf16[288,512]{1,0:T(8,128)(2,1)S(1)}, bf16[288,512]{1,0:T(8,128)(2,1)S(1)}, u32[]{:S(2)}, u32[]{:S(2)}) collective-permute-start(bf16[288,512]{1,0:T(8,128)(2,1)S(1)} %add_convert_fusion.7), channel_id=1, source_target_pairs={{0,8},{1,17},{2,10},{3,19},{4,12},{5,21},{6,14},{7,23},{8,0},{9,25... | collective-permute-start | bytes 884744 | tf_op jit(solution)/shard_map/ppermute | solution.py:995
  117.1 10.9 %collective-permute-start.9 = (bf16[256,768]{1,0:T(8,128)(2,1)S(1)}, bf16[256,768]{1,0:T(8,128)(2,1)S(1)}, u32[]{:S(2)}, u32[]{:S(2)}) collective-permute-start(bf16[256,768]{1,0:T(8,128)(2,1)S(1)} %copy-done.10), channel_id=1, source_target_pairs={{0,2},{1,5},{2,0},{3,7},{4,6},{5,1},{6,4},{7,3},{8,10},{9,13},{10,... | collective-permute-start | bytes 1179656 | tf_op jit(solution)/shard_map/ppermute | solution.py:995
  117.1 10.8 %collective-permute-start.10 = (bf16[288,512]{1,0:T(8,128)(2,1)S(1)}, bf16[288,512]{1,0:T(8,128)(2,1)S(1)}, u32[]{:S(2)}, u32[]{:S(2)}) collective-permute-start(bf16[288,512]{1,0:T(8,128)(2,1)S(1)} %add_convert_fusion.5), channel_id=1, source_target_pairs={{0,16},{1,3},{2,18},{3,1},{4,20},{5,7},{6,22},{7,5},{8,24},{9,11},... | collective-permute-start | bytes 884744 | tf_op jit(solution)/shard_map/ppermute | solution.py:995
  117.1 11.0 %copy-start.5 = (bf16[256,768]{1,0:T(8,128)(2,1)S(1)}, bf16[256,768]{1,0:T(8,128)(2,1)}, u32[]{:S(2)}) copy-start(bf16[256,768]{1,0:T(8,128)(2,1)} %get-tuple-element.207) | copy-start | bytes 1179652
  128.2 9.6 %collective-permute-start.14 = (bf16[1024,512]{1,0:T(8,128)(2,1)}, bf16[1024,512]{1,0:T(8,128)(2,1)S(1)}, u32[]{:S(2)}, u32[]{:S(2)}) collective-permute-start(bf16[1024,512]{1,0:T(8,128)(2,1)} %get-tuple-element.229), channel_id=1, source_target_pairs={{0,1},{1,0},{2,3},{3,2},{4,5},{5,4},{6,7},{7,6},{8,9},{9,8},{10,11... | collective-permute-start | bytes 3145736 | tf_op jit(solution)/shard_map/ppermute | solution.py:949
  128.3 9.5 %collective-permute-start.12 = (bf16[288,512]{1,0:T(8,128)(2,1)S(1)}, bf16[288,512]{1,0:T(8,128)(2,1)S(1)}, u32[]{:S(2)}, u32[]{:S(2)}) collective-permute-start(bf16[288,512]{1,0:T(8,128)(2,1)S(1)} %add_convert_fusion.4), channel_id=1, source_target_pairs={{0,8},{1,17},{2,10},{3,19},{4,12},{5,21},{6,14},{7,23},{8,0},{9,25... | collective-permute-start | bytes 884744 | tf_op jit(solution)/shard_map/ppermute | solution.py:995
  128.4 9.4 %collective-permute-start.13 = (bf16[288,512]{1,0:T(8,128)(2,1)S(1)}, bf16[288,512]{1,0:T(8,128)(2,1)S(1)}, u32[]{:S(2)}, u32[]{:S(2)}) collective-permute-start(bf16[288,512]{1,0:T(8,128)(2,1)S(1)} %add_convert_fusion.4), channel_id=1, source_target_pairs={{0,2},{1,5},{2,0},{3,7},{4,6},{5,1},{6,4},{7,3},{8,10},{9,13},{10,... | collective-permute-start | bytes 884744 | tf_op jit(solution)/shard_map/ppermute | solution.py:995
  130.9 6.9 %collective-permute-start.15 = (bf16[1024,128]{1,0:T(8,128)(2,1)}, bf16[1024,128]{1,0:T(8,128)(2,1)S(1)}, u32[]{:S(2)}, u32[]{:S(2)}) collective-permute-start(bf16[1024,128]{1,0:T(8,128)(2,1)} %get-tuple-element.230), channel_id=1, source_target_pairs={{0,1},{1,0},{2,3},{3,2},{4,5},{5,4},{6,7},{7,6},{8,9},{9,8},{10,11... | collective-permute-start | bytes 786440 | tf_op jit(solution)/shard_map/ppermute | solution.py:949
  130.9 6.9 %collective-permute-start.11 = (bf16[128,768]{1,0:T(8,128)(2,1)S(1)}, bf16[128,768]{1,0:T(8,128)(2,1)S(1)}, u32[]{:S(2)}, u32[]{:S(2)}) collective-permute-start(bf16[128,768]{1,0:T(8,128)(2,1)S(1)} %get-tuple-element.226), channel_id=1, source_target_pairs={{0,4},{1,3},{2,6},{3,1},{4,0},{5,7},{6,2},{7,5},{8,12},{9,11},{10,... | collective-permute-start | bytes 589832 | tf_op jit(solution)/shard_map/ppermute | solution.py:995
  137.8 4.0 %copy-start.6 = (bf16[1024,128]{1,0:T(8,128)(2,1)}, bf16[1024,128]{1,0:T(8,128)(2,1)S(1)}, u32[]{:S(2)}) copy-start(bf16[1024,128]{1,0:T(8,128)(2,1)S(1)} %collective-permute-done.15.arrived_in) | copy-start | bytes 786436
  138.7 9.9 %collective-permute-start.17 = (bf16[576,512]{1,0:T(8,128)(2,1)S(1)}, bf16[576,512]{1,0:T(8,128)(2,1)S(1)}, u32[]{:S(2)}, u32[]{:S(2)}) collective-permute-start(bf16[576,512]{1,0:T(8,128)(2,1)S(1)} %constant_dynamic-update-slice_fusion.3), channel_id=1, source_target_pairs={{0,4},{1,9},{2,6},{3,11},{4,0},{5,13},{6,2},{7,15},{8,12},{9,1},{1... | collective-permute-start | bytes 1769480 | tf_op jit(solution)/shard_map/ppermute | solution.py:995
  140.5 7.0 %collective-permute-start.16 = (bf16[64,768]{1,0:T(8,128)(2,1)}, bf16[64,768]{1,0:T(8,128)(2,1)}, u32[]{:S(2)}, u32[]{:S(2)}) collective-permute-start(bf16[64,768]{1,0:T(8,128)(2,1)} %add_convert_fusion.13), channel_id=1, source_target_pairs={{0,8},{1,9},{2,10},{3,11},{4,12},{5,13},{6,14},{7,15},{8,0},{9,1},... | collective-permute-start | bytes 294920 | tf_op jit(solution)/shard_map/ppermute | solution.py:995
  149.6 10.9 %collective-permute-start.19 = (bf16[432,512]{1,0:T(8,128)(2,1)S(1)}, bf16[432,512]{1,0:T(8,128)(2,1)S(1)}, u32[]{:S(2)}, u32[]{:S(2)}) collective-permute-start(bf16[432,512]{1,0:T(8,128)(2,1)S(1)} %pad_maximum_fusion.7), channel_id=1, source_target_pairs={{0,2},{1,5},{2,0},{3,7},{4,6},{5,1},{6,4},{7,3},{8,10},{9,13},{10,... | collective-permute-start | bytes 1327112 | tf_op jit(solution)/shard_map/ppermute | solution.py:995
  152.2 8.2 %collective-permute-start.18 = (bf16[64,768]{1,0:T(8,128)(2,1)S(1)}, bf16[64,768]{1,0:T(8,128)(2,1)S(1)}, u32[]{:S(2)}, u32[]{:S(2)}) collective-permute-start(bf16[64,768]{1,0:T(8,128)(2,1)S(1)} %add_convert_fusion.11), channel_id=1, source_target_pairs={{0,16},{1,17},{2,18},{3,19},{4,20},{5,21},{6,22},{7,23},{8,24},{9,... | collective-permute-start | bytes 294920 | tf_op jit(solution)/shard_map/ppermute | solution.py:995
  160.5 8.4 %collective-permute-start.21 = (bf16[432,512]{1,0:T(8,128)(2,1)S(1)}, bf16[432,512]{1,0:T(8,128)(2,1)S(1)}, u32[]{:S(2)}, u32[]{:S(2)}) collective-permute-start(bf16[432,512]{1,0:T(8,128)(2,1)S(1)} %slice.13), channel_id=1, source_target_pairs={{0,2},{1,5},{2,0},{3,7},{4,6},{5,1},{6,4},{7,3},{8,10},{9,13},{10,... | collective-permute-start | bytes 1327112 | tf_op jit(solution)/shard_map/ppermute | solution.py:995
  160.6 4.9 %collective-permute-start.20 = (bf16[64,768]{1,0:T(8,128)(2,1)S(1)}, bf16[64,768]{1,0:T(8,128)(2,1)S(1)}, u32[]{:S(2)}, u32[]{:S(2)}) collective-permute-start(bf16[64,768]{1,0:T(8,128)(2,1)S(1)} %add_convert_fusion.10), channel_id=1, source_target_pairs={{0,8},{1,9},{2,10},{3,11},{4,12},{5,13},{6,14},{7,15},{8,0},{9,1},... | collective-permute-start | bytes 294920 | tf_op jit(solution)/shard_map/ppermute | solution.py:995
  169.3 7.6 %collective-permute-start.24 = (bf16[2304,512]{1,0:T(8,128)(2,1)S(1)}, bf16[2304,512]{1,0:T(8,128)(2,1)S(1)}, u32[]{:S(2)}, u32[]{:S(2)}) collective-permute-start(bf16[2304,512]{1,0:T(8,128)(2,1)S(1)} %constant_dynamic-update-slice_fusion.2.refs_0_), channel_id=1, source_target_pairs={{0,1},{1,0},{2,3},{3,2},{4,5},{5,4},{6,7},{7,6},{8,9},{9,8},{10,11... | collective-permute-start | bytes 7077896 | tf_op jit(solution)/shard_map/ppermute | solution.py:949
  169.4 7.5 %collective-permute-start.22 = (bf16[128,768]{1,0:T(8,128)(2,1)S(1)}, bf16[128,768]{1,0:T(8,128)(2,1)S(1)}, u32[]{:S(2)}, u32[]{:S(2)}) collective-permute-start(bf16[128,768]{1,0:T(8,128)(2,1)S(1)} %constant_dynamic-update-slice_fusion.1), channel_id=1, source_target_pairs={{0,4},{1,3},{2,6},{3,1},{4,0},{5,7},{6,2},{7,5},{8,12},{9,11},{10,... | collective-permute-start | bytes 589832 | tf_op jit(solution)/shard_map/ppermute | solution.py:995
  170.0 6.9 %collective-permute-start.23 = (bf16[128,768]{1,0:T(8,128)(2,1)S(1)}, bf16[128,768]{1,0:T(8,128)(2,1)S(1)}, u32[]{:S(2)}, u32[]{:S(2)}) collective-permute-start(bf16[128,768]{1,0:T(8,128)(2,1)S(1)} %constant_dynamic-update-slice_fusion.1), channel_id=1, source_target_pairs={{0,2},{1,5},{2,0},{3,7},{4,6},{5,1},{6,4},{7,3},{8,10},{9,13},{10,... | collective-permute-start | bytes 589832 | tf_op jit(solution)/shard_map/ppermute | solution.py:995
  176.9 5.8 %collective-permute-start.26 = (bf16[256,768]{1,0:T(8,128)(2,1)S(1)}, bf16[256,768]{1,0:T(8,128)(2,1)S(1)}, u32[]{:S(2)}, u32[]{:S(2)}) collective-permute-start(bf16[256,768]{1,0:T(8,128)(2,1)S(1)} %constant_dynamic-update-slice_fusion.6), channel_id=1, source_target_pairs={{0,1},{1,0},{2,3},{3,2},{4,5},{5,4},{6,7},{7,6},{8,9},{9,8},{10,11... | collective-permute-start | bytes 1179656 | tf_op jit(solution)/shard_map/ppermute | solution.py:949
  177.0 5.7 %collective-permute-start.25 = (bf16[128,768]{1,0:T(8,128)(2,1)S(1)}, bf16[128,768]{1,0:T(8,128)(2,1)S(1)}, u32[]{:S(2)}, u32[]{:S(2)}) collective-permute-start(bf16[128,768]{1,0:T(8,128)(2,1)S(1)} %collective-permute-done.22), channel_id=1, source_target_pairs={{0,2},{1,5},{2,0},{3,7},{4,6},{5,1},{6,4},{7,3},{8,10},{9,13},{10,... | collective-permute-start | bytes 589832 | tf_op jit(solution)/shard_map/ppermute | solution.py:995
  182.7 1.8 collective-permute-start.27
  (7 other events, 10.9 us)

commit v2 on v1

--- a/solution.py
+++ b/solution.py
@@ -1074,7 +1074,7 @@
             (self.other,) = yield [(swap_cores, self.mine)]
 
 
-ORDERS = ((0, 1, 2, 3), (1, 2, 3, 0))
+ORDERS = ((0, 1, 2, 3), (1, 0, 3, 2))
 PROJECTION_ORDERS = ((0, 1, 2, 3), (1, 0, 2, 3))
 CUTS = (0, 2, 5, 8)
 

time: 190 us -> 189 us (level)
  transfers between devices with their start and end apart: 28 -> 28, of which waited for: 13 -> 14; matrix products, arithmetic and copies ran while one was open for 1% -> 1% of each run, Pallas kernels for 38% -> 38%
where the time goes in v2:
time: 189 us; the launch traced here: 186 us
  Pallas kernels  121 us (64%)
  waiting for transfers between devices  31.4 us (17%)
  starting transfers between devices  24.1 us (13%)
  local copies, waits for them, and re-layouts  4.02 us (2%)
  other arithmetic  3.87 us (2%)
  between operations  1.98 us (1%)
    pallas_call x11, Pallas kernels, run_kernel(): pl.pallas_call(kernel, in_specs=[smem] * len(scalars) + [large] * len(arg...  121 us
    ppermute x17, waiting for transfers between devices, swap(): return lax.ppermute(array, ('seq', 'head'), pairs)  24.5 us
    ppermute x17, starting transfers between devices, swap(): return lax.ppermute(array, ('seq', 'head'), pairs)  21.5 us
    ppermute x11, waiting for transfers between devices, swap_cores(): return lax.ppermute(array, 'head', [(0, 1), (1, 0)])  6.96 us
  transfers between devices with their start and end apart: 28, of which 14 were waited for; matrix products, arithmetic and copies ran while one was open for 1% of the time, Pallas kernels for 38%

profile of v2, /device:TPU:0, one launch (start us, length us, event | category | flops | bytes accessed | tf_op | source)
XLA Modules:
  0.0 186.0 jit_solution(6720432070016658289)
XLA Ops:
  2.5 1.9 %collective-permute-done.1.skip_other_in = bf16[1024,256]{1,0:T(8,128)(2,1)S(1)} collective-permute-done((bf16[1024,256]{1,0:T(8,128)(2,1)}, bf16[1024,256]{1,0:T(8,128)(2,1)S(1)}, u32[]{:S(2)}, u32[]{:S(2)}) %collective-permute-start.1) | collective-permute-done | bytes 524320 | tf_op jit(solution)/shard_map/ppermute | solution.py:949
  5.6 21.9 %forward_attention.1 = (bf16[1024,256]{1,0:T(8,128)(2,1)}, bf16[1024,256]{1,0:T(8,128)(2,1)}, bf16[2,2048,128]{2,1,0:T(8,128)(2,1)}, bf16[2,2048,128]{2,1,0:T(8,...) custom-call(s32[5]{0:T(128)} %stack.16.info, ...), custom_call_target="tpu_custom_call" | custom-call | flops 10000000000 | bytes 11931648 | tf_op jit(solution)/shard_map/forward_attention/pallas_call | solution.py:250
  27.9 1.7 collective-permute-done.2.mixed_other_in
  30.4 25.7 %row_part.1 = (bf16[1024,512]{1,0:T(8,128)(2,1)}, f32[1024,512]{1,0:T(8,128)}, bf16[1024,256]{1,0:T(8,128)(2,1)}, bf16[1024,256]{1,0:T(8,128)(2,1)}, bf16[1152,5...) custom-call(s32[5]{0:T(128)} %stack.16.info, ...), custom_call_target="tpu_custom_call" | custom-call | flops 15000000512 | bytes 16805888 | tf_op jit(solution)/shard_map/row_part/pallas_call | solution.py:250
  56.5 1.7 collective-permute-done.3.grad_other_in
  59.1 4.6 %arrange_rows.1 = (bf16[2,2048,128]{2,1,0:T(8,128)(2,1)}, f32[2,8,2048]{2,1,0:T(8,128)}) custom-call(s32[5]{0:T(128)} %stack.16.info, bf16[1024,256]{1,0:T(8,128)(2,1)} %get-tuple-element.159.grad_own_in, bf16[1024,256]{1,0:T(8,128)(2,1)} %copy-done.4, bf16[2,2048,128]{2,1,0:T(8,128)(2,1)} %get-tuple-element.163.mixed_in), custom_call_target="tpu_custom_call" | custom-call | flops 100000000 | bytes 3276800 | tf_op jit(solution)/shard_map/arrange_rows/pallas_call | solution.py:250
  65.2 16.6 %blocks_0.1 = (f32[2,2048,128]{2,1,0:T(8,128)}, bf16[512,512]{1,0:T(8,128)(2,1)}) custom-call(s32[5]{0:T(128)} %stack.16.info, bf16[2,2048,128]{2,1,0:T(8,128)(2,1)} %get-tuple-element.196.refs_0_, bf16[2,2048,128]{2,1,0:T(8,128)(2,1)} %get-tuple-element.197.refs_1_, bf16[2,2048,128]{2,1,0:T(8,128)(2,1)} %get-tuple-element.198.refs_2_, ...), custom_call_target="tpu_custom_call" | custom-call | flops 5000000000 | bytes 7077888 | tf_op jit(solution)/shard_map/blocks_0/pallas_call | solution.py:250
  82.3 2.0 %collective-permute-start.7 = (bf16[576,512]{1,0:T(8,128)(2,1)S(1)}, bf16[576,512]{1,0:T(8,128)(2,1)S(1)}, u32[]{:S(2)}, u32[]{:S(2)}) collective-permute-start(bf16[576,512]{1,0:T(8,128)(2,1)S(1)} %add_convert_fusion.3), channel_id=1, source_target_pairs={{0,4},{1,3},{2,6},{3,1},{4,0},{5,7},{6,2},{7,5},{8,12},{9,11},{10,... | collective-permute-start | bytes 1769480 | tf_op jit(solution)/shard_map/ppermute | solution.py:995
  84.3 16.8 %blocks_2.1 = (f32[2,2048,128]{2,1,0:T(8,128)}, bf16[768,512]{1,0:T(8,128)(2,1)}) custom-call(s32[5]{0:T(128)} %stack.16.info, bf16[2,2048,128]{2,1,0:T(8,128)(2,1)} %get-tuple-element.196.refs_0_, bf16[2,2048,128]{2,1,0:T(8,128)(2,1)} %get-tuple-element.197.refs_1_, ...), custom_call_target="tpu_custom_call", output_to_operand_aliasing={{0}: (7, {})} | custom-call | flops 5000000000 | bytes 9437184 | tf_op jit(solution)/shard_map/blocks_2/pallas_call | solution.py:250
  101.4 2.5 %collective-permute-start.8 = (bf16[288,512]{1,0:T(8,128)(2,1)S(1)}, bf16[288,512]{1,0:T(8,128)(2,1)S(1)}, u32[]{:S(2)}, u32[]{:S(2)}) collective-permute-start(bf16[288,512]{1,0:T(8,128)(2,1)S(1)} %add_convert_fusion.7), channel_id=1, source_target_pairs={{0,8},{1,17},{2,10},{3,19},{4,12},{5,21},{6,14},{7,23},{8,0},{9,25... | collective-permute-start | bytes 884744 | tf_op jit(solution)/shard_map/ppermute | solution.py:995
  103.9 13.1 %last_blocks.1 = (bf16[256,768]{1,0:T(8,128)(2,1)}, bf16[256,768]{1,0:T(8,128)(2,1)}, bf16[2048,768]{1,0:T(8,128)(2,1)}) custom-call(s32[5]{0:T(128)} %stack.16.info, bf16[2,2048,128]{2,1,0:T(8,128)(2,1)} %get-tuple-element.196.refs_0_, bf16[2,2048,128]{2,1,0:T(8,128)(2,1)} %get-tuple-element.197.refs_1_, bf16[2,2048,128]{2,1,0:T(8,128)(2,1)} %get-tuple-element.198.refs_2_, ...), custom_call_target="tpu_custom_call" | custom-call | flops 5000000000 | bytes 15224832 | tf_op jit(solution)/shard_map/last_blocks/pallas_call | solution.py:250
  118.0 2.2 %collective-permute-start.10 = (bf16[288,512]{1,0:T(8,128)(2,1)S(1)}, bf16[288,512]{1,0:T(8,128)(2,1)S(1)}, u32[]{:S(2)}, u32[]{:S(2)}) collective-permute-start(bf16[288,512]{1,0:T(8,128)(2,1)S(1)} %add_convert_fusion.5), channel_id=1, source_target_pairs={{0,16},{1,9},{2,18},{3,11},{4,20},{5,13},{6,22},{7,15},{8,24},{9,1... | collective-permute-start | bytes 884744 | tf_op jit(solution)/shard_map/ppermute | solution.py:995
  120.2 7.8 %back_rows.1 = (bf16[1024,512]{1,0:T(8,128)(2,1)}, bf16[1024,512]{1,0:T(8,128)(2,1)}, bf16[1024,128]{1,0:T(8,128)(2,1)}, bf16[1024,128]{1,0:T(8,128)(2,1)}) custom-call(s32[5]{0:T(128)} %stack.16.info, bf16[2048,768]{1,0:T(8,128)(2,1)} %get-tuple-element.217.packed_in, bf16[512,512]{1,0:T(8,128)(2,1)} %query_in.3, bf16[512,512]{1,0:T(8,128)(2,1)} %key_in.3, ...), custom_call_target="tpu_custom_call" | custom-call | flops 2000000000 | bytes 7077888 | tf_op jit(solution)/shard_map/back_rows/pallas_call | solution.py:250
  128.9 2.5 %collective-permute-start.13 = (bf16[288,512]{1,0:T(8,128)(2,1)S(1)}, bf16[288,512]{1,0:T(8,128)(2,1)S(1)}, u32[]{:S(2)}, u32[]{:S(2)}) collective-permute-start(bf16[288,512]{1,0:T(8,128)(2,1)S(1)} %add_convert_fusion.4), channel_id=1, source_target_pairs={{0,2},{1,5},{2,0},{3,7},{4,6},{5,1},{6,4},{7,3},{8,10},{9,13},{10,... | collective-permute-start | bytes 884744 | tf_op jit(solution)/shard_map/ppermute | solution.py:995
  131.5 5.7 %collective-permute-done.11 = bf16[128,768]{1,0:T(8,128)(2,1)S(1)} collective-permute-done((bf16[128,768]{1,0:T(8,128)(2,1)S(1)}, bf16[128,768]{1,0:T(8,128)(2,1)S(1)}, u32[]{:S(2)}, u32[]{:S(2)}) %collective-permute-start.11) | collective-permute-done | bytes 196640 | tf_op jit(solution)/shard_map/ppermute | solution.py:995
  137.2 1.6 collective-permute-done.12
  139.7 1.9 %collective-permute-start.16 = (bf16[64,768]{1,0:T(8,128)(2,1)}, bf16[64,768]{1,0:T(8,128)(2,1)}, u32[]{:S(2)}, u32[]{:S(2)}) collective-permute-start(bf16[64,768]{1,0:T(8,128)(2,1)} %add_convert_fusion.13), channel_id=1, source_target_pairs={{0,8},{1,9},{2,10},{3,11},{4,12},{5,13},{6,14},{7,15},{8,0},{9,1},... | collective-permute-start | bytes 294920 | tf_op jit(solution)/shard_map/ppermute | solution.py:995
  141.6 5.8 %close_rows.1 = (bf16[1024,512]{1,0:T(8,128)(2,1)}, bf16[1024,256]{1,0:T(8,128)(2,1)}) custom-call(s32[5]{0:T(128)} %stack.16.info, bf16[1024,512]{1,0:T(8,128)(2,1)} %tokens_in.3, f32[1024,512]{1,0:T(8,128)} %get-tuple-element.237.after_grad_in, bf16[1024,512]{1,0:T(8,128)(2,1)} %get-tuple-element.238.back_own_in, bf16[1024,512]{1,0:T(8,128)(2,1)} %copy-done.3, ...), custom_call_target="tpu_custom_call" | custom-call | flops 100000000 | bytes 7342080 | tf_op jit(solution)/shard_map/close_rows/pallas_call | solution.py:250
  147.3 2.2 %collective-permute-done.17 = bf16[576,512]{1,0:T(8,128)(2,1)S(1)} collective-permute-done((bf16[576,512]{1,0:T(8,128)(2,1)S(1)}, bf16[576,512]{1,0:T(8,128)(2,1)S(1)}, u32[]{:S(2)}, u32[]{:S(2)}) %collective-permute-start.17) | collective-permute-done | bytes 589856 | tf_op jit(solution)/shard_map/ppermute | solution.py:995
  150.5 2.0 %collective-permute-start.19 = (bf16[432,512]{1,0:T(8,128)(2,1)S(1)}, bf16[432,512]{1,0:T(8,128)(2,1)S(1)}, u32[]{:S(2)}, u32[]{:S(2)}) collective-permute-start(bf16[432,512]{1,0:T(8,128)(2,1)S(1)} %pad_maximum_fusion.7), channel_id=1, source_target_pairs={{0,2},{1,5},{2,0},{3,7},{4,6},{5,1},{6,4},{7,3},{8,10},{9,13},{10,... | collective-permute-start | bytes 1327112 | tf_op jit(solution)/shard_map/ppermute | solution.py:995
  152.6 1.2 collective-permute-start.18
  153.9 5.3 %collective-permute-done.18 = bf16[64,768]{1,0:T(8,128)(2,1)S(1)} collective-permute-done((bf16[64,768]{1,0:T(8,128)(2,1)S(1)}, bf16[64,768]{1,0:T(8,128)(2,1)S(1)}, u32[]{:S(2)}, u32[]{:S(2)}) %collective-permute-start.18) | collective-permute-done | bytes 98336 | tf_op jit(solution)/shard_map/ppermute | solution.py:995
  159.3 1.6 collective-permute-start.21
  162.0 3.6 %collective-permute-done.20 = bf16[64,768]{1,0:T(8,128)(2,1)S(1)} collective-permute-done((bf16[64,768]{1,0:T(8,128)(2,1)S(1)}, bf16[64,768]{1,0:T(8,128)(2,1)S(1)}, u32[]{:S(2)}, u32[]{:S(2)}) %collective-permute-start.20) | collective-permute-done | bytes 98336 | tf_op jit(solution)/shard_map/ppermute | solution.py:995
  165.7 2.0 %collective-permute-done.21 = bf16[432,512]{1,0:T(8,128)(2,1)S(1)} collective-permute-done((bf16[432,512]{1,0:T(8,128)(2,1)S(1)}, bf16[432,512]{1,0:T(8,128)(2,1)S(1)}, u32[]{:S(2)}, u32[]{:S(2)}) %collective-permute-start.21) | collective-permute-done | bytes 442400 | tf_op jit(solution)/shard_map/ppermute | solution.py:995
  168.7 1.5 collective-permute-start.23
  170.2 3.0 %unpack_half.1 = (f32[2048,512]{1,0:T(8,128)}, f32[512,2048]{1,0:T(8,128)}, f32[512,512]{1,0:T(8,128)}) custom-call(s32[5]{0:T(128)S(1)} %copy-done, bf16[2304,512]{1,0:T(8,128)(2,1)S(1)} %constant_dynamic-update-slice_fusion.2.refs_0_), custom_call_target="tpu_custom_call" | custom-call | flops 100000000 | bytes 11796480 | tf_op jit(solution)/shard_map/unpack_half/pallas_call | solution.py:250
  173.3 2.0 %collective-permute-done.22 = bf16[128,768]{1,0:T(8,128)(2,1)S(1)} collective-permute-done((bf16[128,768]{1,0:T(8,128)(2,1)S(1)}, bf16[128,768]{1,0:T(8,128)(2,1)S(1)}, u32[]{:S(2)}, u32[]{:S(2)}) %collective-permute-start.22) | collective-permute-done | bytes 196640 | tf_op jit(solution)/shard_map/ppermute | solution.py:995
  176.0 1.5 collective-permute-start.25
  177.4 3.0 %unpack_late.1 = (f32[2048,512]{1,0:T(8,128)}, f32[512,2048]{1,0:T(8,128)}, f32[512,512]{1,0:T(8,128)}) custom-call(s32[5]{0:T(128)S(1)} %copy-done, bf16[2304,512]{1,0:T(8,128)(2,1)S(1)} %collective-permute-done.24.refs_0_, f32[2048,512]{1,0:T(8,128)} %get-tuple-element.273.refs_1_, ...), custom_call_target="tpu_custom_call", output_to_operand_aliasing={{0}: (2, {}), {1}: (3, {}), {2}: (4, {})} | custom-call | flops 100000000 | bytes 21233664 | tf_op jit(solution)/shard_map/unpack_late/pallas_call | solution.py:250
  181.9 1.5 collective-permute-done.27
  183.5 2.3 %split_projection.1 = (f32[512,512]{1,0:T(8,128)}, f32[512,512]{1,0:T(8,128)}, f32[512,256]{1,0:T(8,128)}, f32[1,512]{1,0:T(1,128)}, f32[1,512]{1,0:T(1,128)}, /...) custom-call(s32[5]{0:T(128)S(1)} %copy-done, ...), custom_call_target="tpu_custom_call" | custom-call | flops 100000000 | bytes 4210688 | tf_op jit(solution)/shard_map/split_projection/pallas_call | solution.py:250
  (92 shorter events, 15.1 us)
Async XLA Ops:
  0.6 3.8 %collective-permute-start = (bf16[1024,512]{1,0:T(8,128)(2,1)}, bf16[1024,512]{1,0:T(8,128)(2,1)S(1)}, u32[]{:S(2)}, u32[]{:S(2)}) collective-permute-start(bf16[1024,512]{1,0:T(8,128)(2,1)} %tokens_in.3), channel_id=1, source_target_pairs={{0,1},{1,0},{2,3},{3,2},{4,5},{5,4},{6,7},{7,6},{8,9},{9,8},{10,11... | collective-permute-start | bytes 3145736 | tf_op jit(solution)/shard_map/ppermute | solution.py:949
  1.2 3.2 %collective-permute-start.1 = (bf16[1024,256]{1,0:T(8,128)(2,1)}, bf16[1024,256]{1,0:T(8,128)(2,1)S(1)}, u32[]{:S(2)}, u32[]{:S(2)}) collective-permute-start(bf16[1024,256]{1,0:T(8,128)(2,1)} %skip_own_in.1), channel_id=1, source_target_pairs={{0,1},{1,0},{2,3},{3,2},{4,5},{5,4},{6,7},{7,6},{8,9},{9,8},{10,11... | collective-permute-start | bytes 1572872 | tf_op jit(solution)/shard_map/ppermute | solution.py:949
  27.4 2.2 %collective-permute-start.2 = (bf16[1024,256]{1,0:T(8,128)(2,1)}, bf16[1024,256]{1,0:T(8,128)(2,1)S(1)}, u32[]{:S(2)}, u32[]{:S(2)}) collective-permute-start(bf16[1024,256]{1,0:T(8,128)(2,1)} %get-tuple-element.154), channel_id=1, source_target_pairs={{0,1},{1,0},{2,3},{3,2},{4,5},{5,4},{6,7},{7,6},{8,9},{9,8},{10,11... | collective-permute-start | bytes 1572872 | tf_op jit(solution)/shard_map/ppermute | solution.py:949
  56.1 7.6 %copy-start.2 = (bf16[1152,512]{1,0:T(8,128)(2,1)S(1)}, bf16[1152,512]{1,0:T(8,128)(2,1)}, u32[]{:S(2)}) copy-start(bf16[1152,512]{1,0:T(8,128)(2,1)} %get-tuple-element.169) | copy-start | bytes 3538948
  56.1 2.2 %collective-permute-start.3 = (bf16[1024,256]{1,0:T(8,128)(2,1)}, bf16[1024,256]{1,0:T(8,128)(2,1)S(1)}, u32[]{:S(2)}, u32[]{:S(2)}) collective-permute-start(bf16[1024,256]{1,0:T(8,128)(2,1)} %get-tuple-element.160), channel_id=1, source_target_pairs={{0,1},{1,0},{2,3},{3,2},{4,5},{5,4},{6,7},{7,6},{8,9},{9,8},{10,11... | collective-permute-start | bytes 1572872 | tf_op jit(solution)/shard_map/ppermute | solution.py:949
  58.3 5.4 %collective-permute-start.4 = (bf16[1152,512]{1,0:T(8,128)(2,1)}, bf16[1152,512]{1,0:T(8,128)(2,1)S(1)}, u32[]{:S(2)}, u32[]{:S(2)}) collective-permute-start(bf16[1152,512]{1,0:T(8,128)(2,1)} %get-tuple-element.165), channel_id=1, source_target_pairs={{0,1},{1,0},{2,3},{3,2},{4,5},{5,4},{6,7},{7,6},{8,9},{9,8},{10,11... | collective-permute-start | bytes 3538952 | tf_op jit(solution)/shard_map/ppermute | solution.py:949
  58.7 23.1 %collective-permute-start.6 = (bf16[1152,512]{1,0:T(8,128)(2,1)}, bf16[1152,512]{1,0:T(8,128)(2,1)S(1)}, u32[]{:S(2)}, u32[]{:S(2)}) collective-permute-start(bf16[1152,512]{1,0:T(8,128)(2,1)} %get-tuple-element.180), channel_id=1, source_target_pairs={{0,1},{1,0},{2,3},{3,2},{4,5},{5,4},{6,7},{7,6},{8,9},{9,8},{10,11... | collective-permute-start | bytes 3538952 | tf_op jit(solution)/shard_map/ppermute | solution.py:949
  64.1 17.7 %collective-permute-start.5 = (bf16[1152,512]{1,0:T(8,128)(2,1)S(1)}, bf16[1152,512]{1,0:T(8,128)(2,1)S(1)}, u32[]{:S(2)}, u32[]{:S(2)}) collective-permute-start(bf16[1152,512]{1,0:T(8,128)(2,1)S(1)} %add_convert_fusion.1), channel_id=1, source_target_pairs={{0,2},{1,5},{2,0},{3,7},{4,6},{5,1},{6,4},{7,3},{8,10},{9,13},{10,... | collective-permute-start | bytes 3538952 | tf_op jit(solution)/shard_map/ppermute | solution.py:995
  65.2 16.7 %copy-start.1 = (bf16[1152,512]{1,0:T(8,128)(2,1)S(1)}, bf16[1152,512]{1,0:T(8,128)(2,1)}, u32[]{:S(2)}) copy-start(bf16[1152,512]{1,0:T(8,128)(2,1)} %get-tuple-element.181) | copy-start | bytes 3538948
  82.3 18.8 %collective-permute-start.7 = (bf16[576,512]{1,0:T(8,128)(2,1)S(1)}, bf16[576,512]{1,0:T(8,128)(2,1)S(1)}, u32[]{:S(2)}, u32[]{:S(2)}) collective-permute-start(bf16[576,512]{1,0:T(8,128)(2,1)S(1)} %add_convert_fusion.3), channel_id=1, source_target_pairs={{0,4},{1,3},{2,6},{3,1},{4,0},{5,7},{6,2},{7,5},{8,12},{9,11},{10,... | collective-permute-start | bytes 1769480 | tf_op jit(solution)/shard_map/ppermute | solution.py:995
  101.4 15.6 %collective-permute-start.8 = (bf16[288,512]{1,0:T(8,128)(2,1)S(1)}, bf16[288,512]{1,0:T(8,128)(2,1)S(1)}, u32[]{:S(2)}, u32[]{:S(2)}) collective-permute-start(bf16[288,512]{1,0:T(8,128)(2,1)S(1)} %add_convert_fusion.7), channel_id=1, source_target_pairs={{0,8},{1,17},{2,10},{3,19},{4,12},{5,21},{6,14},{7,23},{8,0},{9,25... | collective-permute-start | bytes 884744 | tf_op jit(solution)/shard_map/ppermute | solution.py:995
  118.0 10.6 %collective-permute-start.9 = (bf16[256,768]{1,0:T(8,128)(2,1)S(1)}, bf16[256,768]{1,0:T(8,128)(2,1)S(1)}, u32[]{:S(2)}, u32[]{:S(2)}) collective-permute-start(bf16[256,768]{1,0:T(8,128)(2,1)S(1)} %copy-done.10), channel_id=1, source_target_pairs={{0,2},{1,5},{2,0},{3,7},{4,6},{5,1},{6,4},{7,3},{8,10},{9,13},{10,... | collective-permute-start | bytes 1179656 | tf_op jit(solution)/shard_map/ppermute | solution.py:995
  118.0 10.6 %collective-permute-start.10 = (bf16[288,512]{1,0:T(8,128)(2,1)S(1)}, bf16[288,512]{1,0:T(8,128)(2,1)S(1)}, u32[]{:S(2)}, u32[]{:S(2)}) collective-permute-start(bf16[288,512]{1,0:T(8,128)(2,1)S(1)} %add_convert_fusion.5), channel_id=1, source_target_pairs={{0,16},{1,9},{2,18},{3,11},{4,20},{5,13},{6,22},{7,15},{8,24},{9,1... | collective-permute-start | bytes 884744 | tf_op jit(solution)/shard_map/ppermute | solution.py:995
  120.2 8.5 %copy-start.5 = (bf16[256,768]{1,0:T(8,128)(2,1)S(1)}, bf16[256,768]{1,0:T(8,128)(2,1)}, u32[]{:S(2)}) copy-start(bf16[256,768]{1,0:T(8,128)(2,1)} %get-tuple-element.207) | copy-start | bytes 1179652
  128.8 10.0 %collective-permute-start.14 = (bf16[1024,512]{1,0:T(8,128)(2,1)}, bf16[1024,512]{1,0:T(8,128)(2,1)S(1)}, u32[]{:S(2)}, u32[]{:S(2)}) collective-permute-start(bf16[1024,512]{1,0:T(8,128)(2,1)} %get-tuple-element.229), channel_id=1, source_target_pairs={{0,1},{1,0},{2,3},{3,2},{4,5},{5,4},{6,7},{7,6},{8,9},{9,8},{10,11... | collective-permute-start | bytes 3145736 | tf_op jit(solution)/shard_map/ppermute | solution.py:949
  128.9 9.9 %collective-permute-start.12 = (bf16[288,512]{1,0:T(8,128)(2,1)S(1)}, bf16[288,512]{1,0:T(8,128)(2,1)S(1)}, u32[]{:S(2)}, u32[]{:S(2)}) collective-permute-start(bf16[288,512]{1,0:T(8,128)(2,1)S(1)} %add_convert_fusion.4), channel_id=1, source_target_pairs={{0,8},{1,17},{2,10},{3,19},{4,12},{5,21},{6,14},{7,23},{8,0},{9,25... | collective-permute-start | bytes 884744 | tf_op jit(solution)/shard_map/ppermute | solution.py:995
  128.9 9.9 %collective-permute-start.13 = (bf16[288,512]{1,0:T(8,128)(2,1)S(1)}, bf16[288,512]{1,0:T(8,128)(2,1)S(1)}, u32[]{:S(2)}, u32[]{:S(2)}) collective-permute-start(bf16[288,512]{1,0:T(8,128)(2,1)S(1)} %add_convert_fusion.4), channel_id=1, source_target_pairs={{0,2},{1,5},{2,0},{3,7},{4,6},{5,1},{6,4},{7,3},{8,10},{9,13},{10,... | collective-permute-start | bytes 884744 | tf_op jit(solution)/shard_map/ppermute | solution.py:995
  131.4 5.8 %collective-permute-start.15 = (bf16[1024,128]{1,0:T(8,128)(2,1)}, bf16[1024,128]{1,0:T(8,128)(2,1)S(1)}, u32[]{:S(2)}, u32[]{:S(2)}) collective-permute-start(bf16[1024,128]{1,0:T(8,128)(2,1)} %get-tuple-element.230), channel_id=1, source_target_pairs={{0,1},{1,0},{2,3},{3,2},{4,5},{5,4},{6,7},{7,6},{8,9},{9,8},{10,11... | collective-permute-start | bytes 786440 | tf_op jit(solution)/shard_map/ppermute | solution.py:949
  131.4 5.8 %collective-permute-start.11 = (bf16[128,768]{1,0:T(8,128)(2,1)S(1)}, bf16[128,768]{1,0:T(8,128)(2,1)S(1)}, u32[]{:S(2)}, u32[]{:S(2)}) collective-permute-start(bf16[128,768]{1,0:T(8,128)(2,1)S(1)} %get-tuple-element.226), channel_id=1, source_target_pairs={{0,4},{1,3},{2,6},{3,1},{4,0},{5,7},{6,2},{7,5},{8,12},{9,11},{10,... | collective-permute-start | bytes 589832 | tf_op jit(solution)/shard_map/ppermute | solution.py:995
  137.2 4.3 %copy-start.6 = (bf16[1024,128]{1,0:T(8,128)(2,1)}, bf16[1024,128]{1,0:T(8,128)(2,1)S(1)}, u32[]{:S(2)}) copy-start(bf16[1024,128]{1,0:T(8,128)(2,1)S(1)} %collective-permute-done.15.arrived_in) | copy-start | bytes 786436
  139.6 9.9 %collective-permute-start.17 = (bf16[576,512]{1,0:T(8,128)(2,1)S(1)}, bf16[576,512]{1,0:T(8,128)(2,1)S(1)}, u32[]{:S(2)}, u32[]{:S(2)}) collective-permute-start(bf16[576,512]{1,0:T(8,128)(2,1)S(1)} %constant_dynamic-update-slice_fusion.3), channel_id=1, source_target_pairs={{0,4},{1,3},{2,6},{3,1},{4,0},{5,7},{6,2},{7,5},{8,12},{9,11},{10,... | collective-permute-start | bytes 1769480 | tf_op jit(solution)/shard_map/ppermute | solution.py:995
  139.7 7.6 %collective-permute-start.16 = (bf16[64,768]{1,0:T(8,128)(2,1)}, bf16[64,768]{1,0:T(8,128)(2,1)}, u32[]{:S(2)}, u32[]{:S(2)}) collective-permute-start(bf16[64,768]{1,0:T(8,128)(2,1)} %add_convert_fusion.13), channel_id=1, source_target_pairs={{0,8},{1,9},{2,10},{3,11},{4,12},{5,13},{6,14},{7,15},{8,0},{9,1},... | collective-permute-start | bytes 294920 | tf_op jit(solution)/shard_map/ppermute | solution.py:995
  150.5 8.7 %collective-permute-start.19 = (bf16[432,512]{1,0:T(8,128)(2,1)S(1)}, bf16[432,512]{1,0:T(8,128)(2,1)S(1)}, u32[]{:S(2)}, u32[]{:S(2)}) collective-permute-start(bf16[432,512]{1,0:T(8,128)(2,1)S(1)} %pad_maximum_fusion.7), channel_id=1, source_target_pairs={{0,2},{1,5},{2,0},{3,7},{4,6},{5,1},{6,4},{7,3},{8,10},{9,13},{10,... | collective-permute-start | bytes 1327112 | tf_op jit(solution)/shard_map/ppermute | solution.py:995
  152.6 6.6 %collective-permute-start.18 = (bf16[64,768]{1,0:T(8,128)(2,1)S(1)}, bf16[64,768]{1,0:T(8,128)(2,1)S(1)}, u32[]{:S(2)}, u32[]{:S(2)}) collective-permute-start(bf16[64,768]{1,0:T(8,128)(2,1)S(1)} %add_convert_fusion.11), channel_id=1, source_target_pairs={{0,16},{1,17},{2,18},{3,19},{4,20},{5,21},{6,22},{7,23},{8,24},{9,... | collective-permute-start | bytes 294920 | tf_op jit(solution)/shard_map/ppermute | solution.py:995
  159.3 8.4 %collective-permute-start.21 = (bf16[432,512]{1,0:T(8,128)(2,1)S(1)}, bf16[432,512]{1,0:T(8,128)(2,1)S(1)}, u32[]{:S(2)}, u32[]{:S(2)}) collective-permute-start(bf16[432,512]{1,0:T(8,128)(2,1)S(1)} %slice.13), channel_id=1, source_target_pairs={{0,2},{1,5},{2,0},{3,7},{4,6},{5,1},{6,4},{7,3},{8,10},{9,13},{10,... | collective-permute-start | bytes 1327112 | tf_op jit(solution)/shard_map/ppermute | solution.py:995
  161.0 4.7 %collective-permute-start.20 = (bf16[64,768]{1,0:T(8,128)(2,1)S(1)}, bf16[64,768]{1,0:T(8,128)(2,1)S(1)}, u32[]{:S(2)}, u32[]{:S(2)}) collective-permute-start(bf16[64,768]{1,0:T(8,128)(2,1)S(1)} %add_convert_fusion.10), channel_id=1, source_target_pairs={{0,8},{1,9},{2,10},{3,11},{4,12},{5,13},{6,14},{7,15},{8,0},{9,1},... | collective-permute-start | bytes 294920 | tf_op jit(solution)/shard_map/ppermute | solution.py:995
  168.1 7.4 %collective-permute-start.24 = (bf16[2304,512]{1,0:T(8,128)(2,1)S(1)}, bf16[2304,512]{1,0:T(8,128)(2,1)S(1)}, u32[]{:S(2)}, u32[]{:S(2)}) collective-permute-start(bf16[2304,512]{1,0:T(8,128)(2,1)S(1)} %constant_dynamic-update-slice_fusion.2.refs_0_), channel_id=1, source_target_pairs={{0,1},{1,0},{2,3},{3,2},{4,5},{5,4},{6,7},{7,6},{8,9},{9,8},{10,11... | collective-permute-start | bytes 7077896 | tf_op jit(solution)/shard_map/ppermute | solution.py:949
  168.2 7.1 %collective-permute-start.22 = (bf16[128,768]{1,0:T(8,128)(2,1)S(1)}, bf16[128,768]{1,0:T(8,128)(2,1)S(1)}, u32[]{:S(2)}, u32[]{:S(2)}) collective-permute-start(bf16[128,768]{1,0:T(8,128)(2,1)S(1)} %constant_dynamic-update-slice_fusion.1), channel_id=1, source_target_pairs={{0,4},{1,3},{2,6},{3,1},{4,0},{5,7},{6,2},{7,5},{8,12},{9,11},{10,... | collective-permute-start | bytes 589832 | tf_op jit(solution)/shard_map/ppermute | solution.py:995
  168.7 6.8 %collective-permute-start.23 = (bf16[128,768]{1,0:T(8,128)(2,1)S(1)}, bf16[128,768]{1,0:T(8,128)(2,1)S(1)}, u32[]{:S(2)}, u32[]{:S(2)}) collective-permute-start(bf16[128,768]{1,0:T(8,128)(2,1)S(1)} %constant_dynamic-update-slice_fusion.1), channel_id=1, source_target_pairs={{0,2},{1,5},{2,0},{3,7},{4,6},{5,1},{6,4},{7,3},{8,10},{9,13},{10,... | collective-permute-start | bytes 589832 | tf_op jit(solution)/shard_map/ppermute | solution.py:995
  175.5 6.1 %collective-permute-start.26 = (bf16[256,768]{1,0:T(8,128)(2,1)S(1)}, bf16[256,768]{1,0:T(8,128)(2,1)S(1)}, u32[]{:S(2)}, u32[]{:S(2)}) collective-permute-start(bf16[256,768]{1,0:T(8,128)(2,1)S(1)} %constant_dynamic-update-slice_fusion.6), channel_id=1, source_target_pairs={{0,1},{1,0},{2,3},{3,2},{4,5},{5,4},{6,7},{7,6},{8,9},{9,8},{10,11... | collective-permute-start | bytes 1179656 | tf_op jit(solution)/shard_map/ppermute | solution.py:949
  176.0 5.7 %collective-permute-start.25 = (bf16[128,768]{1,0:T(8,128)(2,1)S(1)}, bf16[128,768]{1,0:T(8,128)(2,1)S(1)}, u32[]{:S(2)}, u32[]{:S(2)}) collective-permute-start(bf16[128,768]{1,0:T(8,128)(2,1)S(1)} %collective-permute-done.22), channel_id=1, source_target_pairs={{0,2},{1,5},{2,0},{3,7},{4,6},{5,1},{6,4},{7,3},{8,10},{9,13},{10,... | collective-permute-start | bytes 589832 | tf_op jit(solution)/shard_map/ppermute | solution.py:995
  181.7 1.8 collective-permute-start.27
  (7 other events, 9.5 us)

commit v3 on v2

--- a/solution.py
+++ b/solution.py
@@ -1129,7 +1129,7 @@
             packed, sums.coming, sums.mine, sums.kept = after_all(packed, sums.coming, sums.mine, sums.kept)
     projection.begin(projection_stay, None, projection_away, None)
 
-    lanes = [projection.flow(True, True), sums.flow(False, False)]
+    lanes = [sums.flow(False, False), projection.flow(True, True)]
     pending = [next(lane) for lane in lanes]
     work, made, extra, finished = 0, None, (), False
     while pending:

time: 189 us -> 189 us (level)
  transfers between devices with their start and end apart: 28 -> 28, of which waited for: 14 -> 15; matrix products, arithmetic and copies ran while one was open for 1% -> 1% of each run, Pallas kernels for 38% -> 38%
where the time goes in v3:
time: 189 us; the launch traced here: 186 us
  Pallas kernels  121 us (64%)
  waiting for transfers between devices  30.3 us (16%)
  starting transfers between devices  25 us (13%)
  local copies, waits for them, and re-layouts  4.02 us (2%)
  other arithmetic  3.86 us (2%)
  between operations  1.98 us (1%)
    pallas_call x11, Pallas kernels, run_kernel(): pl.pallas_call(kernel, in_specs=[smem] * len(scalars) + [large] * len(arg...  121 us
    ppermute x17, waiting for transfers between devices, swap(): return lax.ppermute(array, ('seq', 'head'), pairs)  23.3 us
    ppermute x17, starting transfers between devices, swap(): return lax.ppermute(array, ('seq', 'head'), pairs)  22.5 us
    ppermute x11, waiting for transfers between devices, swap_cores(): return lax.ppermute(array, 'head', [(0, 1), (1, 0)])  6.96 us
  transfers between devices with their start and end apart: 28, of which 15 were waited for; matrix products, arithmetic and copies ran while one was open for 1% of the time, Pallas kernels for 38%

profile of v3, /device:TPU:0, one launch (start us, length us, event | category | flops | bytes accessed | tf_op | source)
XLA Modules:
  0.0 185.8 jit_solution(6720432070016658289)
XLA Ops:
  2.5 1.9 %collective-permute-done.1.skip_other_in = bf16[1024,256]{1,0:T(8,128)(2,1)S(1)} collective-permute-done((bf16[1024,256]{1,0:T(8,128)(2,1)}, bf16[1024,256]{1,0:T(8,128)(2,1)S(1)}, u32[]{:S(2)}, u32[]{:S(2)}) %collective-permute-start.1) | collective-permute-done | bytes 524320 | tf_op jit(solution)/shard_map/ppermute | solution.py:949
  5.6 21.9 %forward_attention.1 = (bf16[1024,256]{1,0:T(8,128)(2,1)}, bf16[1024,256]{1,0:T(8,128)(2,1)}, bf16[2,2048,128]{2,1,0:T(8,128)(2,1)}, bf16[2,2048,128]{2,1,0:T(8,...) custom-call(s32[5]{0:T(128)} %stack.16.info, ...), custom_call_target="tpu_custom_call" | custom-call | flops 10000000000 | bytes 11931648 | tf_op jit(solution)/shard_map/forward_attention/pallas_call | solution.py:250
  27.9 1.7 collective-permute-done.2.mixed_other_in
  30.4 25.7 %row_part.1 = (bf16[1024,512]{1,0:T(8,128)(2,1)}, f32[1024,512]{1,0:T(8,128)}, bf16[1024,256]{1,0:T(8,128)(2,1)}, bf16[1024,256]{1,0:T(8,128)(2,1)}, bf16[1152,5...) custom-call(s32[5]{0:T(128)} %stack.16.info, ...), custom_call_target="tpu_custom_call" | custom-call | flops 15000000512 | bytes 16805888 | tf_op jit(solution)/shard_map/row_part/pallas_call | solution.py:250
  56.5 1.7 collective-permute-done.3.grad_other_in
  59.1 4.6 %arrange_rows.1 = (bf16[2,2048,128]{2,1,0:T(8,128)(2,1)}, f32[2,8,2048]{2,1,0:T(8,128)}) custom-call(s32[5]{0:T(128)} %stack.16.info, bf16[1024,256]{1,0:T(8,128)(2,1)} %get-tuple-element.159.grad_own_in, bf16[1024,256]{1,0:T(8,128)(2,1)} %copy-done.4, bf16[2,2048,128]{2,1,0:T(8,128)(2,1)} %get-tuple-element.163.mixed_in), custom_call_target="tpu_custom_call" | custom-call | flops 100000000 | bytes 3276800 | tf_op jit(solution)/shard_map/arrange_rows/pallas_call | solution.py:250
  64.1 1.1 collective-permute-start.5
  65.2 16.6 %blocks_0.1 = (f32[2,2048,128]{2,1,0:T(8,128)}, bf16[512,512]{1,0:T(8,128)(2,1)}) custom-call(s32[5]{0:T(128)} %stack.16.info, bf16[2,2048,128]{2,1,0:T(8,128)(2,1)} %get-tuple-element.196.refs_0_, bf16[2,2048,128]{2,1,0:T(8,128)(2,1)} %get-tuple-element.197.refs_1_, bf16[2,2048,128]{2,1,0:T(8,128)(2,1)} %get-tuple-element.198.refs_2_, ...), custom_call_target="tpu_custom_call" | custom-call | flops 5000000000 | bytes 7077888 | tf_op jit(solution)/shard_map/blocks_0/pallas_call | solution.py:250
  82.4 16.8 %blocks_2.1 = (f32[2,2048,128]{2,1,0:T(8,128)}, bf16[768,512]{1,0:T(8,128)(2,1)}) custom-call(s32[5]{0:T(128)} %stack.16.info, bf16[2,2048,128]{2,1,0:T(8,128)(2,1)} %get-tuple-element.196.refs_0_, bf16[2,2048,128]{2,1,0:T(8,128)(2,1)} %get-tuple-element.197.refs_1_, ...), custom_call_target="tpu_custom_call", output_to_operand_aliasing={{0}: (7, {})} | custom-call | flops 5000000000 | bytes 9437184 | tf_op jit(solution)/shard_map/blocks_2/pallas_call | solution.py:250
  99.5 2.5 %collective-permute-start.8 = (bf16[288,512]{1,0:T(8,128)(2,1)S(1)}, bf16[288,512]{1,0:T(8,128)(2,1)S(1)}, u32[]{:S(2)}, u32[]{:S(2)}) collective-permute-start(bf16[288,512]{1,0:T(8,128)(2,1)S(1)} %add_convert_fusion.7), channel_id=1, source_target_pairs={{0,8},{1,17},{2,10},{3,19},{4,12},{5,21},{6,14},{7,23},{8,0},{9,25... | collective-permute-start | bytes 884744 | tf_op jit(solution)/shard_map/ppermute | solution.py:995
  102.0 13.1 %last_blocks.1 = (bf16[256,768]{1,0:T(8,128)(2,1)}, bf16[256,768]{1,0:T(8,128)(2,1)}, bf16[2048,768]{1,0:T(8,128)(2,1)}) custom-call(s32[5]{0:T(128)} %stack.16.info, bf16[2,2048,128]{2,1,0:T(8,128)(2,1)} %get-tuple-element.196.refs_0_, bf16[2,2048,128]{2,1,0:T(8,128)(2,1)} %get-tuple-element.197.refs_1_, bf16[2,2048,128]{2,1,0:T(8,128)(2,1)} %get-tuple-element.198.refs_2_, ...), custom_call_target="tpu_custom_call" | custom-call | flops 5000000000 | bytes 15224832 | tf_op jit(solution)/shard_map/last_blocks/pallas_call | solution.py:250
  116.1 4.1 %collective-permute-start.9 = (bf16[288,512]{1,0:T(8,128)(2,1)S(1)}, bf16[288,512]{1,0:T(8,128)(2,1)S(1)}, u32[]{:S(2)}, u32[]{:S(2)}) collective-permute-start(bf16[288,512]{1,0:T(8,128)(2,1)S(1)} %add_convert_fusion.5), channel_id=1, source_target_pairs={{0,16},{1,9},{2,18},{3,11},{4,20},{5,13},{6,22},{7,15},{8,24},{9,1... | collective-permute-start | bytes 884744 | tf_op jit(solution)/shard_map/ppermute | solution.py:995
  120.2 7.8 %back_rows.1 = (bf16[1024,512]{1,0:T(8,128)(2,1)}, bf16[1024,512]{1,0:T(8,128)(2,1)}, bf16[1024,128]{1,0:T(8,128)(2,1)}, bf16[1024,128]{1,0:T(8,128)(2,1)}) custom-call(s32[5]{0:T(128)} %stack.16.info, bf16[2048,768]{1,0:T(8,128)(2,1)} %get-tuple-element.216.packed_in, bf16[512,512]{1,0:T(8,128)(2,1)} %query_in.3, bf16[512,512]{1,0:T(8,128)(2,1)} %key_in.3, ...), custom_call_target="tpu_custom_call" | custom-call | flops 2000000000 | bytes 7077888 | tf_op jit(solution)/shard_map/back_rows/pallas_call | solution.py:250
  128.4 1.9 %collective-permute-start.11 = (bf16[288,512]{1,0:T(8,128)(2,1)S(1)}, bf16[288,512]{1,0:T(8,128)(2,1)S(1)}, u32[]{:S(2)}, u32[]{:S(2)}) collective-permute-start(bf16[288,512]{1,0:T(8,128)(2,1)S(1)} %add_convert_fusion.4), channel_id=1, source_target_pairs={{0,8},{1,17},{2,10},{3,19},{4,12},{5,21},{6,14},{7,23},{8,0},{9,25... | collective-permute-start | bytes 884744 | tf_op jit(solution)/shard_map/ppermute | solution.py:995
  130.3 1.6 collective-permute-start.12
  132.0 6.0 %collective-permute-done.13 = bf16[128,768]{1,0:T(8,128)(2,1)S(1)} collective-permute-done((bf16[128,768]{1,0:T(8,128)(2,1)S(1)}, bf16[128,768]{1,0:T(8,128)(2,1)S(1)}, u32[]{:S(2)}, u32[]{:S(2)}) %collective-permute-start.13) | collective-permute-done | bytes 196640 | tf_op jit(solution)/shard_map/ppermute | solution.py:995
  139.8 1.6 collective-permute-start.16
  142.0 5.8 %close_rows.1 = (bf16[1024,512]{1,0:T(8,128)(2,1)}, bf16[1024,256]{1,0:T(8,128)(2,1)}) custom-call(s32[5]{0:T(128)} %stack.16.info, bf16[1024,512]{1,0:T(8,128)(2,1)} %tokens_in.3, f32[1024,512]{1,0:T(8,128)} %get-tuple-element.237.after_grad_in, bf16[1024,512]{1,0:T(8,128)(2,1)} %get-tuple-element.238.back_own_in, bf16[1024,512]{1,0:T(8,128)(2,1)} %copy-done.3, ...), custom_call_target="tpu_custom_call" | custom-call | flops 100000000 | bytes 7342080 | tf_op jit(solution)/shard_map/close_rows/pallas_call | solution.py:250
  147.8 1.9 %collective-permute-done.16 = bf16[576,512]{1,0:T(8,128)(2,1)S(1)} collective-permute-done((bf16[576,512]{1,0:T(8,128)(2,1)S(1)}, bf16[576,512]{1,0:T(8,128)(2,1)S(1)}, u32[]{:S(2)}, u32[]{:S(2)}) %collective-permute-start.16) | collective-permute-done | bytes 589856 | tf_op jit(solution)/shard_map/ppermute | solution.py:995
  150.7 1.8 collective-permute-start.18
  153.6 5.4 %collective-permute-done.19 = bf16[64,768]{1,0:T(8,128)(2,1)S(1)} collective-permute-done((bf16[64,768]{1,0:T(8,128)(2,1)S(1)}, bf16[64,768]{1,0:T(8,128)(2,1)S(1)}, u32[]{:S(2)}, u32[]{:S(2)}) %collective-permute-start.19) | collective-permute-done | bytes 98336 | tf_op jit(solution)/shard_map/ppermute | solution.py:995
  159.1 1.8 collective-permute-start.20
  161.5 4.1 %collective-permute-done.21 = bf16[64,768]{1,0:T(8,128)(2,1)S(1)} collective-permute-done((bf16[64,768]{1,0:T(8,128)(2,1)S(1)}, bf16[64,768]{1,0:T(8,128)(2,1)S(1)}, u32[]{:S(2)}, u32[]{:S(2)}) %collective-permute-start.21) | collective-permute-done | bytes 98336 | tf_op jit(solution)/shard_map/ppermute | solution.py:995
  165.6 1.9 %collective-permute-done.20 = bf16[432,512]{1,0:T(8,128)(2,1)S(1)} collective-permute-done((bf16[432,512]{1,0:T(8,128)(2,1)S(1)}, bf16[432,512]{1,0:T(8,128)(2,1)S(1)}, u32[]{:S(2)}, u32[]{:S(2)}) %collective-permute-start.20) | collective-permute-done | bytes 442400 | tf_op jit(solution)/shard_map/ppermute | solution.py:995
  168.0 1.7 collective-permute-start.23
  170.5 3.0 %unpack_half.1 = (f32[2048,512]{1,0:T(8,128)}, f32[512,2048]{1,0:T(8,128)}, f32[512,512]{1,0:T(8,128)}) custom-call(s32[5]{0:T(128)S(1)} %copy-done, bf16[2304,512]{1,0:T(8,128)(2,1)S(1)} %constant_dynamic-update-slice_fusion.2.refs_0_), custom_call_target="tpu_custom_call" | custom-call | flops 100000000 | bytes 11796480 | tf_op jit(solution)/shard_map/unpack_half/pallas_call | solution.py:250
  173.5 1.4 collective-permute-done.23
  175.7 1.5 collective-permute-start.25
  177.2 3.0 %unpack_late.1 = (f32[2048,512]{1,0:T(8,128)}, f32[512,2048]{1,0:T(8,128)}, f32[512,512]{1,0:T(8,128)}) custom-call(s32[5]{0:T(128)S(1)} %copy-done, bf16[2304,512]{1,0:T(8,128)(2,1)S(1)} %collective-permute-done.22.refs_0_, f32[2048,512]{1,0:T(8,128)} %get-tuple-element.273.refs_1_, ...), custom_call_target="tpu_custom_call", output_to_operand_aliasing={{0}: (2, {}), {1}: (3, {}), {2}: (4, {})} | custom-call | flops 100000000 | bytes 21233664 | tf_op jit(solution)/shard_map/unpack_late/pallas_call | solution.py:250
  180.3 1.1 collective-permute-done.25
  181.7 1.5 collective-permute-done.27
  183.3 2.3 %split_projection.1 = (f32[512,512]{1,0:T(8,128)}, f32[512,512]{1,0:T(8,128)}, f32[512,256]{1,0:T(8,128)}, f32[1,512]{1,0:T(1,128)}, f32[1,512]{1,0:T(1,128)}, /...) custom-call(s32[5]{0:T(128)S(1)} %copy-done, ...), custom_call_target="tpu_custom_call" | custom-call | flops 100000000 | bytes 4210688 | tf_op jit(solution)/shard_map/split_projection/pallas_call | solution.py:250
  (92 shorter events, 14.9 us)
Async XLA Ops:
  0.6 3.8 %collective-permute-start = (bf16[1024,512]{1,0:T(8,128)(2,1)}, bf16[1024,512]{1,0:T(8,128)(2,1)S(1)}, u32[]{:S(2)}, u32[]{:S(2)}) collective-permute-start(bf16[1024,512]{1,0:T(8,128)(2,1)} %tokens_in.3), channel_id=1, source_target_pairs={{0,1},{1,0},{2,3},{3,2},{4,5},{5,4},{6,7},{7,6},{8,9},{9,8},{10,11... | collective-permute-start | bytes 3145736 | tf_op jit(solution)/shard_map/ppermute | solution.py:949
  1.2 3.2 %collective-permute-start.1 = (bf16[1024,256]{1,0:T(8,128)(2,1)}, bf16[1024,256]{1,0:T(8,128)(2,1)S(1)}, u32[]{:S(2)}, u32[]{:S(2)}) collective-permute-start(bf16[1024,256]{1,0:T(8,128)(2,1)} %skip_own_in.1), channel_id=1, source_target_pairs={{0,1},{1,0},{2,3},{3,2},{4,5},{5,4},{6,7},{7,6},{8,9},{9,8},{10,11... | collective-permute-start | bytes 1572872 | tf_op jit(solution)/shard_map/ppermute | solution.py:949
  27.4 2.2 %collective-permute-start.2 = (bf16[1024,256]{1,0:T(8,128)(2,1)}, bf16[1024,256]{1,0:T(8,128)(2,1)S(1)}, u32[]{:S(2)}, u32[]{:S(2)}) collective-permute-start(bf16[1024,256]{1,0:T(8,128)(2,1)} %get-tuple-element.154), channel_id=1, source_target_pairs={{0,1},{1,0},{2,3},{3,2},{4,5},{5,4},{6,7},{7,6},{8,9},{9,8},{10,11... | collective-permute-start | bytes 1572872 | tf_op jit(solution)/shard_map/ppermute | solution.py:949
  56.1 7.6 %copy-start.2 = (bf16[1152,512]{1,0:T(8,128)(2,1)S(1)}, bf16[1152,512]{1,0:T(8,128)(2,1)}, u32[]{:S(2)}) copy-start(bf16[1152,512]{1,0:T(8,128)(2,1)} %get-tuple-element.169) | copy-start | bytes 3538948
  56.1 2.2 %collective-permute-start.3 = (bf16[1024,256]{1,0:T(8,128)(2,1)}, bf16[1024,256]{1,0:T(8,128)(2,1)S(1)}, u32[]{:S(2)}, u32[]{:S(2)}) collective-permute-start(bf16[1024,256]{1,0:T(8,128)(2,1)} %get-tuple-element.160), channel_id=1, source_target_pairs={{0,1},{1,0},{2,3},{3,2},{4,5},{5,4},{6,7},{7,6},{8,9},{9,8},{10,11... | collective-permute-start | bytes 1572872 | tf_op jit(solution)/shard_map/ppermute | solution.py:949
  58.3 5.4 %collective-permute-start.4 = (bf16[1152,512]{1,0:T(8,128)(2,1)}, bf16[1152,512]{1,0:T(8,128)(2,1)S(1)}, u32[]{:S(2)}, u32[]{:S(2)}) collective-permute-start(bf16[1152,512]{1,0:T(8,128)(2,1)} %get-tuple-element.165), channel_id=1, source_target_pairs={{0,1},{1,0},{2,3},{3,2},{4,5},{5,4},{6,7},{7,6},{8,9},{9,8},{10,11... | collective-permute-start | bytes 3538952 | tf_op jit(solution)/shard_map/ppermute | solution.py:949
  58.7 23.1 %collective-permute-start.6 = (bf16[1152,512]{1,0:T(8,128)(2,1)}, bf16[1152,512]{1,0:T(8,128)(2,1)S(1)}, u32[]{:S(2)}, u32[]{:S(2)}) collective-permute-start(bf16[1152,512]{1,0:T(8,128)(2,1)} %get-tuple-element.180), channel_id=1, source_target_pairs={{0,1},{1,0},{2,3},{3,2},{4,5},{5,4},{6,7},{7,6},{8,9},{9,8},{10,11... | collective-permute-start | bytes 3538952 | tf_op jit(solution)/shard_map/ppermute | solution.py:949
  64.1 17.7 %collective-permute-start.5 = (bf16[1152,512]{1,0:T(8,128)(2,1)S(1)}, bf16[1152,512]{1,0:T(8,128)(2,1)S(1)}, u32[]{:S(2)}, u32[]{:S(2)}) collective-permute-start(bf16[1152,512]{1,0:T(8,128)(2,1)S(1)} %add_convert_fusion.1), channel_id=1, source_target_pairs={{0,2},{1,5},{2,0},{3,7},{4,6},{5,1},{6,4},{7,3},{8,10},{9,13},{10,... | collective-permute-start | bytes 3538952 | tf_op jit(solution)/shard_map/ppermute | solution.py:995
  65.2 16.7 %copy-start.1 = (bf16[1152,512]{1,0:T(8,128)(2,1)S(1)}, bf16[1152,512]{1,0:T(8,128)(2,1)}, u32[]{:S(2)}) copy-start(bf16[1152,512]{1,0:T(8,128)(2,1)} %get-tuple-element.181) | copy-start | bytes 3538948
  82.3 16.9 %collective-permute-start.7 = (bf16[576,512]{1,0:T(8,128)(2,1)S(1)}, bf16[576,512]{1,0:T(8,128)(2,1)S(1)}, u32[]{:S(2)}, u32[]{:S(2)}) collective-permute-start(bf16[576,512]{1,0:T(8,128)(2,1)S(1)} %add_convert_fusion.3), channel_id=1, source_target_pairs={{0,4},{1,3},{2,6},{3,1},{4,0},{5,7},{6,2},{7,5},{8,12},{9,11},{10,... | collective-permute-start | bytes 1769480 | tf_op jit(solution)/shard_map/ppermute | solution.py:995
  99.5 15.6 %collective-permute-start.8 = (bf16[288,512]{1,0:T(8,128)(2,1)S(1)}, bf16[288,512]{1,0:T(8,128)(2,1)S(1)}, u32[]{:S(2)}, u32[]{:S(2)}) collective-permute-start(bf16[288,512]{1,0:T(8,128)(2,1)S(1)} %add_convert_fusion.7), channel_id=1, source_target_pairs={{0,8},{1,17},{2,10},{3,19},{4,12},{5,21},{6,14},{7,23},{8,0},{9,25... | collective-permute-start | bytes 884744 | tf_op jit(solution)/shard_map/ppermute | solution.py:995
  116.1 12.0 %collective-permute-start.10 = (bf16[256,768]{1,0:T(8,128)(2,1)S(1)}, bf16[256,768]{1,0:T(8,128)(2,1)S(1)}, u32[]{:S(2)}, u32[]{:S(2)}) collective-permute-start(bf16[256,768]{1,0:T(8,128)(2,1)S(1)} %copy-done.10), channel_id=1, source_target_pairs={{0,2},{1,5},{2,0},{3,7},{4,6},{5,1},{6,4},{7,3},{8,10},{9,13},{10,... | collective-permute-start | bytes 1179656 | tf_op jit(solution)/shard_map/ppermute | solution.py:995
  116.1 12.0 %collective-permute-start.9 = (bf16[288,512]{1,0:T(8,128)(2,1)S(1)}, bf16[288,512]{1,0:T(8,128)(2,1)S(1)}, u32[]{:S(2)}, u32[]{:S(2)}) collective-permute-start(bf16[288,512]{1,0:T(8,128)(2,1)S(1)} %add_convert_fusion.5), channel_id=1, source_target_pairs={{0,16},{1,9},{2,18},{3,11},{4,20},{5,13},{6,22},{7,15},{8,24},{9,1... | collective-permute-start | bytes 884744 | tf_op jit(solution)/shard_map/ppermute | solution.py:995
  120.2 8.0 %copy-start.5 = (bf16[256,768]{1,0:T(8,128)(2,1)S(1)}, bf16[256,768]{1,0:T(8,128)(2,1)}, u32[]{:S(2)}) copy-start(bf16[256,768]{1,0:T(8,128)(2,1)} %get-tuple-element.222) | copy-start | bytes 1179652
  128.3 10.7 %collective-permute-start.14 = (bf16[1024,512]{1,0:T(8,128)(2,1)}, bf16[1024,512]{1,0:T(8,128)(2,1)S(1)}, u32[]{:S(2)}, u32[]{:S(2)}) collective-permute-start(bf16[1024,512]{1,0:T(8,128)(2,1)} %get-tuple-element.229), channel_id=1, source_target_pairs={{0,1},{1,0},{2,3},{3,2},{4,5},{5,4},{6,7},{7,6},{8,9},{9,8},{10,11... | collective-permute-start | bytes 3145736 | tf_op jit(solution)/shard_map/ppermute | solution.py:949
  128.4 9.9 %collective-permute-start.11 = (bf16[288,512]{1,0:T(8,128)(2,1)S(1)}, bf16[288,512]{1,0:T(8,128)(2,1)S(1)}, u32[]{:S(2)}, u32[]{:S(2)}) collective-permute-start(bf16[288,512]{1,0:T(8,128)(2,1)S(1)} %add_convert_fusion.4), channel_id=1, source_target_pairs={{0,8},{1,17},{2,10},{3,19},{4,12},{5,21},{6,14},{7,23},{8,0},{9,25... | collective-permute-start | bytes 884744 | tf_op jit(solution)/shard_map/ppermute | solution.py:995
  130.3 8.7 %collective-permute-start.12 = (bf16[288,512]{1,0:T(8,128)(2,1)S(1)}, bf16[288,512]{1,0:T(8,128)(2,1)S(1)}, u32[]{:S(2)}, u32[]{:S(2)}) collective-permute-start(bf16[288,512]{1,0:T(8,128)(2,1)S(1)} %add_convert_fusion.4), channel_id=1, source_target_pairs={{0,2},{1,5},{2,0},{3,7},{4,6},{5,1},{6,4},{7,3},{8,10},{9,13},{10,... | collective-permute-start | bytes 884744 | tf_op jit(solution)/shard_map/ppermute | solution.py:995
  131.9 6.0 %collective-permute-start.15 = (bf16[1024,128]{1,0:T(8,128)(2,1)}, bf16[1024,128]{1,0:T(8,128)(2,1)S(1)}, u32[]{:S(2)}, u32[]{:S(2)}) collective-permute-start(bf16[1024,128]{1,0:T(8,128)(2,1)} %get-tuple-element.230), channel_id=1, source_target_pairs={{0,1},{1,0},{2,3},{3,2},{4,5},{5,4},{6,7},{7,6},{8,9},{9,8},{10,11... | collective-permute-start | bytes 786440 | tf_op jit(solution)/shard_map/ppermute | solution.py:949
  131.9 6.0 %collective-permute-start.13 = (bf16[128,768]{1,0:T(8,128)(2,1)S(1)}, bf16[128,768]{1,0:T(8,128)(2,1)S(1)}, u32[]{:S(2)}, u32[]{:S(2)}) collective-permute-start(bf16[128,768]{1,0:T(8,128)(2,1)S(1)} %get-tuple-element.228), channel_id=1, source_target_pairs={{0,4},{1,3},{2,6},{3,1},{4,0},{5,7},{6,2},{7,5},{8,12},{9,11},{10,... | collective-permute-start | bytes 589832 | tf_op jit(solution)/shard_map/ppermute | solution.py:995
  138.0 4.0 %copy-start.6 = (bf16[1024,128]{1,0:T(8,128)(2,1)}, bf16[1024,128]{1,0:T(8,128)(2,1)S(1)}, u32[]{:S(2)}) copy-start(bf16[1024,128]{1,0:T(8,128)(2,1)S(1)} %collective-permute-done.15.arrived_in) | copy-start | bytes 786436
  139.8 9.9 %collective-permute-start.16 = (bf16[576,512]{1,0:T(8,128)(2,1)S(1)}, bf16[576,512]{1,0:T(8,128)(2,1)S(1)}, u32[]{:S(2)}, u32[]{:S(2)}) collective-permute-start(bf16[576,512]{1,0:T(8,128)(2,1)S(1)} %constant_dynamic-update-slice_fusion.4), channel_id=1, source_target_pairs={{0,4},{1,3},{2,6},{3,1},{4,0},{5,7},{6,2},{7,5},{8,12},{9,11},{10,... | collective-permute-start | bytes 1769480 | tf_op jit(solution)/shard_map/ppermute | solution.py:995
  141.4 6.3 %collective-permute-start.17 = (bf16[64,768]{1,0:T(8,128)(2,1)}, bf16[64,768]{1,0:T(8,128)(2,1)}, u32[]{:S(2)}, u32[]{:S(2)}) collective-permute-start(bf16[64,768]{1,0:T(8,128)(2,1)} %add_convert_fusion.13), channel_id=1, source_target_pairs={{0,8},{1,9},{2,10},{3,11},{4,12},{5,13},{6,14},{7,15},{8,0},{9,1},... | collective-permute-start | bytes 294920 | tf_op jit(solution)/shard_map/ppermute | solution.py:995
  150.7 8.4 %collective-permute-start.18 = (bf16[432,512]{1,0:T(8,128)(2,1)S(1)}, bf16[432,512]{1,0:T(8,128)(2,1)S(1)}, u32[]{:S(2)}, u32[]{:S(2)}) collective-permute-start(bf16[432,512]{1,0:T(8,128)(2,1)S(1)} %pad_maximum_fusion.7), channel_id=1, source_target_pairs={{0,2},{1,5},{2,0},{3,7},{4,6},{5,1},{6,4},{7,3},{8,10},{9,13},{10,... | collective-permute-start | bytes 1327112 | tf_op jit(solution)/shard_map/ppermute | solution.py:995
  152.6 6.5 %collective-permute-start.19 = (bf16[64,768]{1,0:T(8,128)(2,1)S(1)}, bf16[64,768]{1,0:T(8,128)(2,1)S(1)}, u32[]{:S(2)}, u32[]{:S(2)}) collective-permute-start(bf16[64,768]{1,0:T(8,128)(2,1)S(1)} %add_convert_fusion.11), channel_id=1, source_target_pairs={{0,16},{1,17},{2,18},{3,19},{4,20},{5,21},{6,22},{7,23},{8,24},{9,... | collective-permute-start | bytes 294920 | tf_op jit(solution)/shard_map/ppermute | solution.py:995
  159.1 8.4 %collective-permute-start.20 = (bf16[432,512]{1,0:T(8,128)(2,1)S(1)}, bf16[432,512]{1,0:T(8,128)(2,1)S(1)}, u32[]{:S(2)}, u32[]{:S(2)}) collective-permute-start(bf16[432,512]{1,0:T(8,128)(2,1)S(1)} %slice.13), channel_id=1, source_target_pairs={{0,2},{1,5},{2,0},{3,7},{4,6},{5,1},{6,4},{7,3},{8,10},{9,13},{10,... | collective-permute-start | bytes 1327112 | tf_op jit(solution)/shard_map/ppermute | solution.py:995
  160.9 4.7 %collective-permute-start.21 = (bf16[64,768]{1,0:T(8,128)(2,1)S(1)}, bf16[64,768]{1,0:T(8,128)(2,1)S(1)}, u32[]{:S(2)}, u32[]{:S(2)}) collective-permute-start(bf16[64,768]{1,0:T(8,128)(2,1)S(1)} %add_convert_fusion.10), channel_id=1, source_target_pairs={{0,8},{1,9},{2,10},{3,11},{4,12},{5,13},{6,14},{7,15},{8,0},{9,1},... | collective-permute-start | bytes 294920 | tf_op jit(solution)/shard_map/ppermute | solution.py:995
  167.9 7.5 %collective-permute-start.22 = (bf16[2304,512]{1,0:T(8,128)(2,1)S(1)}, bf16[2304,512]{1,0:T(8,128)(2,1)S(1)}, u32[]{:S(2)}, u32[]{:S(2)}) collective-permute-start(bf16[2304,512]{1,0:T(8,128)(2,1)S(1)} %constant_dynamic-update-slice_fusion.2.refs_0_), channel_id=1, source_target_pairs={{0,1},{1,0},{2,3},{3,2},{4,5},{5,4},{6,7},{7,6},{8,9},{9,8},{10,11... | collective-permute-start | bytes 7077896 | tf_op jit(solution)/shard_map/ppermute | solution.py:949
  168.0 7.0 %collective-permute-start.23 = (bf16[128,768]{1,0:T(8,128)(2,1)S(1)}, bf16[128,768]{1,0:T(8,128)(2,1)S(1)}, u32[]{:S(2)}, u32[]{:S(2)}) collective-permute-start(bf16[128,768]{1,0:T(8,128)(2,1)S(1)} %constant_dynamic-update-slice_fusion.1), channel_id=1, source_target_pairs={{0,4},{1,3},{2,6},{3,1},{4,0},{5,7},{6,2},{7,5},{8,12},{9,11},{10,... | collective-permute-start | bytes 589832 | tf_op jit(solution)/shard_map/ppermute | solution.py:995
  169.7 5.7 %collective-permute-start.24 = (bf16[128,768]{1,0:T(8,128)(2,1)S(1)}, bf16[128,768]{1,0:T(8,128)(2,1)S(1)}, u32[]{:S(2)}, u32[]{:S(2)}) collective-permute-start(bf16[128,768]{1,0:T(8,128)(2,1)S(1)} %constant_dynamic-update-slice_fusion.1), channel_id=1, source_target_pairs={{0,2},{1,5},{2,0},{3,7},{4,6},{5,1},{6,4},{7,3},{8,10},{9,13},{10,... | collective-permute-start | bytes 589832 | tf_op jit(solution)/shard_map/ppermute | solution.py:995
  175.4 6.0 %collective-permute-start.26 = (bf16[256,768]{1,0:T(8,128)(2,1)S(1)}, bf16[256,768]{1,0:T(8,128)(2,1)S(1)}, u32[]{:S(2)}, u32[]{:S(2)}) collective-permute-start(bf16[256,768]{1,0:T(8,128)(2,1)S(1)} %constant_dynamic-update-slice_fusion.5), channel_id=1, source_target_pairs={{0,1},{1,0},{2,3},{3,2},{4,5},{5,4},{6,7},{7,6},{8,9},{9,8},{10,11... | collective-permute-start | bytes 1179656 | tf_op jit(solution)/shard_map/ppermute | solution.py:949
  175.7 5.7 %collective-permute-start.25 = (bf16[128,768]{1,0:T(8,128)(2,1)S(1)}, bf16[128,768]{1,0:T(8,128)(2,1)S(1)}, u32[]{:S(2)}, u32[]{:S(2)}) collective-permute-start(bf16[128,768]{1,0:T(8,128)(2,1)S(1)} %collective-permute-done.23), channel_id=1, source_target_pairs={{0,2},{1,5},{2,0},{3,7},{4,6},{5,1},{6,4},{7,3},{8,10},{9,13},{10,... | collective-permute-start | bytes 589832 | tf_op jit(solution)/shard_map/ppermute | solution.py:995
  181.4 1.8 collective-permute-start.27
  (7 other events, 10.2 us)
